TPU v7x, 256 devices: a whole 4x4x8 slice. The times are simulated.
256 devices in a mesh: ctx: 16 (over x, z_hi, core), dp: 16 (over z_lo, y).
Axes of the slice: x: 4, y: 4, z: 8 (z_hi: 2, z_lo: 4; z = z_hi * 4 + z_lo), core: 2. Of those that a mesh axis runs over, the one named last changes fastest.
Arguments:
- query_proj: bfloat16 [16, 2048, 4096], P('dp', 'ctx'), may hold values from -6 to 6
- key_proj: bfloat16 [16, 2048, 4096], P('dp', 'ctx'), may hold values from -6 to 6
- value_proj: bfloat16 [16, 2048, 4096], P('dp', 'ctx'), may hold values from -6 to 6
- short_taps: float32 [3, 7, 4096], replicated, may hold values from -2.4 to 2.4
- filter_taps: float32 [256, 128], replicated, may hold values from -0.54 to 0.54
- skip_gain: float32 [4096], replicated, may hold values from -1 to 1
- doc_lengths: int32 [16, 8], P('dp'), may hold values from 1 to 1024, 2048 in all within a row
- out_grad: bfloat16 [16, 2048, 4096], P('dp', 'ctx'), may hold values from -6 to 6
Outputs:
- mixed: bfloat16 [16, 2048, 4096], P('dp', 'ctx')
- grad_query: bfloat16 [16, 2048, 4096], P('dp', 'ctx')
- grad_key: bfloat16 [16, 2048, 4096], P('dp', 'ctx')
- grad_value: bfloat16 [16, 2048, 4096], P('dp', 'ctx')
- grad_short: float32 [3, 7, 4096], replicated
- grad_filter: float32 [256, 128], replicated
- grad_skip: float32 [4096], replicated
Inputs may be any that keep to these rules, and one draw needn't show every extreme that they name: `doc_lengths`: each row holds the lengths of the 8 documents of one context in order; they sum to 2048 and the longest is exactly half of 2048.
All inputs are finite; a program needn't handle non-finite values.
Results may differ from a plain program's by a relative error of at most 0.007.
Values may be sent and summed in bfloat16 or wider, within the bound.
A program may use at most 320 MiB of HBM per device.

v0:
```python
import math

import jax
import jax.numpy as jnp
from jax import lax
from jax.sharding import PartitionSpec as P


def from_behind(value, axis, steps):
    count = lax.axis_size(axis)
    leading, last = (max(0, -steps), min(count, count - steps))
    return lax.ppermute(value, axis, [(source, source + steps) for source in range(leading, last)])


def toeplitz(taps):
    groups, length = taps.shape
    pattern = jnp.concatenate(
        [
            jnp.zeros((groups, 1), taps.dtype),
            taps[:, ::-1],
            jnp.zeros((groups, length), taps.dtype),
        ],
        axis=1,
    )
    tiled = jnp.tile(pattern, (1, length))[:, : 2 * length * length]
    return tiled.reshape(groups, length, 2 * length)


def diagonal_sums(dmat):
    groups, length, double = dmat.shape
    flat = dmat.reshape(groups, length * double)
    flat = jnp.pad(flat, ((0, 0), (0, length)))
    folded = jnp.sum(flat.reshape(groups, length, double + 1), axis=1)
    return folded[:, 1 : length + 1][:, ::-1]


def doc_index(starts, positions):
    return jnp.sum((positions[:, None] >= starts[None, :]).astype(jnp.int32), axis=1) - 1


def featurize(extended, kernel, doc_window, number):
    margin = kernel.shape[0] - 1
    own_docs = doc_window[margin:]
    result = jnp.zeros((number, extended.shape[1]), jnp.float32)
    for offset in range(kernel.shape[0]):
        matches = (doc_window[margin - offset : margin - offset + number] == own_docs).astype(
            jnp.float32
        )
        result = (
            result
            + kernel[offset][None, :]
            * extended[margin - offset : margin - offset + number]
            * matches[:, None]
        )
    return result


def featurize_back(grad_window, kernel, doc_window, number):
    own_docs = doc_window[:number]
    result = jnp.zeros((number, grad_window.shape[1]), jnp.float32)
    for offset in range(kernel.shape[0]):
        matches = (doc_window[offset : offset + number] == own_docs).astype(jnp.float32)
        result = (
            result
            + kernel[offset][None, :] * grad_window[offset : offset + number] * matches[:, None]
        )
    return result


def tap_grads(gradient, extended, doc_window, number, count_taps):
    margin = count_taps - 1
    own_docs = doc_window[margin:]
    result = []
    for offset in range(count_taps):
        matches = (doc_window[margin - offset : margin - offset + number] == own_docs).astype(
            jnp.float32
        )
        result.append(
            jnp.sum(
                gradient * extended[margin - offset : margin - offset + number] * matches[:, None],
                axis=0,
            )
        )
    return jnp.stack(result)


def channels_first(rows, groups, group_width):
    return rows.reshape(rows.shape[0], groups, group_width).transpose(1, 2, 0)


def rows_first(columns):
    groups, group_width, count = columns.shape
    return columns.transpose(2, 0, 1).reshape(count, groups * group_width)


def shards(
    query_proj, key_proj, value_proj, short_taps, filter_taps, skip_gain, doc_lengths, out_grad
):
    query = query_proj[0]
    keys = key_proj[0]
    values = value_proj[0]
    tokens, width = query.shape
    groups, filter_len = filter_taps.shape
    group_width = width // groups
    count_taps = short_taps.shape[1]
    margin = count_taps - 1
    blocks = tokens // filter_len
    reach = filter_len + margin
    anchor = lax.axis_index("ctx") * tokens
    lengths = doc_lengths[0]
    starts = jnp.cumsum(lengths) - lengths
    edge_docs = doc_index(starts, anchor - reach + jnp.arange(tokens + reach, dtype=jnp.int32))
    window_docs = edge_docs[margin:]
    feat_docs = edge_docs[filter_len:]
    target_docs = doc_index(starts, anchor + jnp.arange(tokens + filter_len, dtype=jnp.int32))
    prior_q, prior_k, prior_v = from_behind(
        (query[-margin:], keys[-margin:], values[-margin:]), "ctx", 1
    )
    q_ext = jnp.concatenate([prior_q, query], 0).astype(jnp.float32)
    k_ext = jnp.concatenate([prior_k, keys], 0).astype(jnp.float32)
    v_ext = jnp.concatenate([prior_v, values], 0).astype(jnp.float32)
    q_feat = featurize(q_ext, short_taps[0], feat_docs, tokens)
    k_feat = featurize(k_ext, short_taps[1], feat_docs, tokens)
    v_feat = featurize(v_ext, short_taps[2], feat_docs, tokens)
    u_local = (k_feat * v_feat).astype(jnp.bfloat16)
    u_prior = from_behind(u_local, "ctx", 1)
    u_window = jnp.concatenate([u_prior, u_local], 0)
    u_float = u_local.astype(jnp.float32)
    gradient = out_grad[0].astype(jnp.float32)
    dz = gradient * q_feat
    dz_b = dz.astype(jnp.bfloat16)
    dz_next = from_behind(dz_b, "ctx", -1)
    taps_b = filter_taps.astype(jnp.bfloat16)
    mats = toeplitz(taps_b)
    u_cols = channels_first(u_window, groups, group_width)
    dz_cols = channels_first(dz_b, groups, group_width)
    du_parts = [
        jnp.zeros((groups, group_width, filter_len), jnp.float32) for index in range(blocks + 1)
    ]
    index = 0
    lower = index * filter_len
    mask = target_docs[lower : lower + filter_len][:, None] == window_docs[None, :]
    masked = mats * mask.astype(jnp.bfloat16)[None]
    conv_parts = jnp.einsum("gtj,gfj->gft", masked, u_cols, preferred_element_type=jnp.float32)
    contrib = jnp.einsum("gtj,gft->gfj", masked, dz_cols, preferred_element_type=jnp.float32)
    du_parts[index] = contrib[:, :, :filter_len]
    du_parts[index + 1] = contrib[:, :, filter_len:]
    dmat = (
        jnp.einsum("gft,gfj->gtj", dz_cols, u_cols, preferred_element_type=jnp.float32)
        * mask.astype(jnp.float32)[None]
    )
    filter_local = diagonal_sums(dmat)
    lower = tokens
    edge_mask = (
        target_docs[lower : lower + filter_len][:, None]
        == window_docs[lower : lower + filter_len][None, :]
    )
    edge_mats = mats[:, :, :filter_len] * edge_mask.astype(jnp.bfloat16)[None]
    next_cols = channels_first(dz_next, groups, group_width)
    du_parts[blocks] = du_parts[blocks] + jnp.einsum(
        "gtj,gft->gfj", edge_mats, next_cols, preferred_element_type=jnp.float32
    )
    conv = rows_first(conv_parts)
    total = conv + skip_gain[None, :] * u_float
    mixed = (q_feat * total).astype(jnp.bfloat16)
    dq_feat = gradient * total
    du_conv = rows_first(jnp.concatenate(du_parts[1:], axis=2))
    du_total = du_conv + skip_gain[None, :] * dz
    dk_feat = du_total * v_feat
    dv_feat = du_total * k_feat
    next_q, next_k, next_v = (
        from_behind(dq_feat[:margin].astype(jnp.bfloat16), "ctx", -1).astype(jnp.float32),
        from_behind(dk_feat[:margin].astype(jnp.bfloat16), "ctx", -1).astype(jnp.float32),
        from_behind(dv_feat[:margin].astype(jnp.bfloat16), "ctx", -1).astype(jnp.float32),
    )
    back_docs = target_docs[: tokens + margin]
    grad_query = featurize_back(
        jnp.concatenate([dq_feat, next_q], 0), short_taps[0], back_docs, tokens
    ).astype(jnp.bfloat16)
    grad_key = featurize_back(
        jnp.concatenate([dk_feat, next_k], 0), short_taps[1], back_docs, tokens
    ).astype(jnp.bfloat16)
    grad_value = featurize_back(
        jnp.concatenate([dv_feat, next_v], 0), short_taps[2], back_docs, tokens
    ).astype(jnp.bfloat16)
    short_local = jnp.stack(
        [
            tap_grads(dq_feat, q_ext, feat_docs, tokens, count_taps),
            tap_grads(dk_feat, k_ext, feat_docs, tokens, count_taps),
            tap_grads(dv_feat, v_ext, feat_docs, tokens, count_taps),
        ]
    )
    skip_local = jnp.sum(dz * u_float, axis=0)
    short_sum, filter_sum, skip_sum = lax.psum(
        (short_local, filter_local, skip_local), ("ctx", "dp")
    )
    scale = 1.0 / math.sqrt(tokens * lax.axis_size("ctx") * lax.axis_size("dp"))
    return (
        mixed[None],
        grad_query[None],
        grad_key[None],
        grad_value[None],
        short_sum * scale,
        filter_sum * scale,
        skip_sum * scale,
    )


def solution(mesh):
    return jax.shard_map(
        shards,
        mesh=mesh,
        in_specs=(
            P("dp", "ctx", None),
            P("dp", "ctx", None),
            P("dp", "ctx", None),
            P(),
            P(),
            P(),
            P("dp", None),
            P("dp", "ctx", None),
        ),
        out_specs=(
            P("dp", "ctx", None),
            P("dp", "ctx", None),
            P("dp", "ctx", None),
            P("dp", "ctx", None),
            P(),
            P(),
            P(),
        ),
        check_vma=False,
    )
```

profile of v0, /device:TPU:1, one launch (start us, length us, event | category | flops | bytes accessed | tf_op | source)
XLA Modules:
  0.0 748.3 jit_solution(1525401281453257760)
XLA Ops:
  7.2 1.6 slice_bitcast_fusion
  8.9 10.2 %collective-permute-start.2 = (bf16[6,4096]{1,0:T(8,128)(2,1)}, bf16[6,4096]{1,0:T(8,128)(2,1)}, u32[]{:S(2)}, u32[]{:S(2)}) collective-permute-start(bf16[6,4096]{1,0:T(8,128)(2,1)} %slice_bitcast_fusion), channel_id=1, source_target_pairs={{0,16},{16,32},{32,48},{48,64},{64,80},{80,96},{96,112},{112,128},... | collective-permute-start | bytes 147464 | tf_op jit(solution)/shard_map/ppermute | solution.py:12
  19.1 1.5 slice_bitcast_fusion.1
  20.6 1.9 collective-permute-start.1
  22.5 1.5 slice_bitcast_fusion.2
  24.0 1.9 collective-permute-start
  25.9 1.6 fusion.88
  27.5 3.0 fusion.87
  30.6 0.8 reduce-window_clone.1
  33.0 0.9 convert_element_type.182
  37.0 1.6 copy.61
  38.7 2.3 copy.65
  41.0 6.2 tile.4
  47.2 19.2 %tile.10 = bf16[256,32896]{0,1:T(8,128)(2,1)} reshape(bf16[256,128,257]{0,2,1:T(8,128)(2,1)} %tile.4) | data formatting | bytes 33685504 | tf_op jit(solution)/shard_map/tile | solution.py:25
  66.4 13.8 %slice.548 = bf16[256,32768]{0,1:T(8,128)(2,1)} slice(bf16[256,32896]{0,1:T(8,128)(2,1)} %tile.10), slice={[0:256], [0:32768]} | slice | bytes 33554432 | tf_op jit(solution)/shard_map/slice | solution.py:25
  80.2 23.1 %copy.64 = bf16[256,128,256]{2,1,0:T(8,128)(2,1)} copy(bf16[256,128,256]{0,2,1:T(8,128)(2,1)} %bitcast.122) | data formatting | bytes 33554432 | tf_op jit(solution)/shard_map/reshape | solution.py:26
  103.3 2.2 copy.62
  105.5 4.0 maximum_convert_fusion.2
  109.5 1.4 copy.60
  110.9 2.7 maximum_convert_fusion.1
  113.6 1.4 copy.58
  115.2 2.7 maximum_convert_fusion
  118.1 36.8 %fusion.5 = (f32[4096]{0:T(1024)S(1)}, bf16[128,4096]{0,1:T(8,128)(2,1)}, f32[128,4096]{0,1:T(8,128)}, f32[128,4096]{0,1:T(8,128)}, f32[128,4096]{0,1:T(8,128)S(1)}) fusion(bf16[1,128,4096]{1,2,0:T(8,128)(2,1)} %copy.65, f32[128]{0:T(128)S(1)} %copy-done.37, f32[134,4096]{0,1:T(8,128)} %maximum_convert_fusion.2, f32[4096]{0:T(1024)S(1)} %bitcast.174, ...), kind=kLoop, calls=%fused_computation.42 | loop fusion | flops 33550336 | bytes 52792320 | tf_op jit(solution)/shard_map/reduce_sum | solution.py:193
  154.9 1.9 collective-permute-start.3
  156.9 14.0 %broadcast_multiply_fusion.1 = bf16[256,128,256]{2,1,0:T(8,128)(2,1)} fusion(bf16[256,128,256]{2,1,0:T(8,128)(2,1)} %copy.64, bf16[128,256]{1,0:T(8,128)(2,1)S(1)} %get-tuple-element.89), kind=kLoop, calls=%fused_computation.5 | loop fusion | flops 8388608 | bytes 33619968 | tf_op jit(solution)/shard_map/mul | solution.py:143
  171.1 79.8 %psum.23 = f32[4096]{0:T(1024)S(1)} all-reduce(f32[4096]{0:T(1024)S(1)} %get-tuple-element.51), channel_id=1, replica_groups=mesh['ctx'=16,'dp'=16] {'ctx','dp'}, use_global_device_ids=true, to_apply=%region_28.29 | all-reduce | flops 4096 | bytes 32768 | tf_op jit(solution)/shard_map/psum | solution.py:194
  251.6 3.1 pad_maximum_fusion.3
  254.7 12.2 %fusion.90 = f32[256,16,128]{2,1,0:T(8,128)} fusion(bf16[256,16,256]{2,1,0:T(8,128)(2,1)} %bitcast.123, bf16[256,128,256]{2,1,0:T(8,128)(2,1)} %broadcast_multiply_fusion.1), kind=kOutput, calls=%fused_computation.192 | convolution fusion | flops 268435456 | bytes 20971520 | tf_op jit(solution)/shard_map/gtj,gfj->gft/dot_general | solution.py:144
  266.9 19.8 %multiply_reduce_fusion.14 = (f32[4096]{0:T(1024)S(1)}, f32[4096]{0:T(1024)S(1)}, f32[4096]{0:T(1024)S(1)}, f32[4096]{0:T(1024)S(1)}, f32[4096]{0:T(1024)S(1)}, ...) fusion(f32[134,4096]{0,1:T(8,128)} %maximum_convert_fusion, ...), kind=kLoop, calls=%fused_computation.140 | loop fusion | flops 15175680 | bytes 25299968 | tf_op jit(solution)/shard_map/reduce_sum | solution.py:79
  286.7 1.3 copy-done.5
  288.0 1.1 slice.941
  289.1 1.6 copy.66
  290.7 2.6 collective-permute-start.4
  293.3 2.4 collective-permute-start.5
  295.8 17.6 %broadcast_multiply_fusion = f32[256,128,256]{2,1,0:T(8,128)} fusion(f32[128,256]{1,0:T(8,128)S(1)} %copy-done.10, bf16[256,16,128]{2,1,0:T(8,128)(2,1)} %bitcast.125, bf16[256,16,256]{2,1,0:T(8,128)(2,1)} %bitcast.124), kind=kOutput, calls=%fused_computation | convolution fusion | flops 276824064 | bytes 36831232 | tf_op jit(solution)/shard_map/gft,gfj->gtj/dot_general | solution.py:149
  313.4 7.1 fusion.1
  320.4 2.4 copy.74
  322.8 35.0 %copy.79 = f32[256,128,256]{0,2,1:T(8,128)} copy(f32[256,128,256]{2,1,0:T(8,128)} %broadcast_multiply_fusion) | data formatting | bytes 67108864 | tf_op jit(solution)/shard_map/reshape | solution.py:31
  357.8 22.5 %pad.4 = f32[256,32896]{0,1:T(8,128)} pad(f32[256,32768]{0,1:T(8,128)} %bitcast.121, f32[]{:T(128)} %constant.32.clone.1), padding=0_0x0_128 | pad | bytes 67239936 | tf_op jit(solution)/shard_map/jit(_pad)/pad | solution.py:32
  380.3 28.3 %reshape.202 = f32[256,128,257]{0,2,1:T(8,128)} reshape(f32[256,32896]{0,1:T(8,128)} %pad.4) | data formatting | bytes 67371008 | tf_op jit(solution)/shard_map/reshape | solution.py:33
  408.7 11.8 %reduce_sum.248 = f32[256,257]{0,1:T(8,128)S(1)} reduce(f32[256,128,257]{0,2,1:T(8,128)} %reshape.202, f32[]{:T(128)} %constant.32.clone.1), dimensions={1}, to_apply=%region_25.26 | reduce | flops 8355584 | bytes 33948676 | tf_op jit(solution)/shard_map/reduce_sum | solution.py:33
  421.4 1.7 copy.67
  423.1 18.9 %fusion.79 = bf16[1,128,4096]{1,2,0:T(8,128)(2,1)} fusion(f32[128]{0:T(128)S(1)} %get-tuple-element.93, f32[6,4096]{0,1:T(8,128)} %copy.67, f32[128,4096]{0,1:T(8,128)} %copy-done.5, f32[4096]{0:T(1024)S(1)} %bitcast.161, f32[128]{0:T(128)S(1)} %get-tuple-element.94, f32[4096]{0:T(1024)S(1)} %bitcast.163, f32[128]{0:T(128)S(1)} %get-tuple-element.95, ...), kind=kLoop, calls=%fused_computation.153 | loop fusion | flops 13631488 | bytes 3361792 | tf_op jit(solution)/shard_map/broadcast_in_dim | solution.py:200
  442.1 2.3 copy.75
  444.3 8.1 %fusion.78 = f32[256,16,128]{2,1,0:T(8,128)} fusion(f32[256,16,128]{2,1,0:T(8,128)} %fusion.1, bf16[256,16,128]{2,1,0:T(8,128)(2,1)} %bitcast.40, bf16[256,128,256]{2,1,0:T(8,128)(2,1)} %copy.64, bf16[128,128]{1,0:T(8,128)(2,1)S(1)} %compare_convert_fusion.2), kind=kOutput, calls=%fused_computation.152 | convolution fusion | flops 138936320 | bytes 13664256 | tf_op jit(solution)/shard_map/gtj,gft->gfj/dot_general | solution.py:160
  452.4 11.6 %multiply_reduce_fusion = (f32[4096]{0:T(1024)S(1)}, f32[4096]{0:T(1024)S(1)}, f32[4096]{0:T(1024)S(1)}, f32[4096]{0:T(1024)S(1)}, f32[4096]{0:T(1024)S(1)}, /*i...) fusion(f32[134,4096]{0,1:T(8,128)S(1)} %copy-done.1, f32[128]{0:T(128)S(1)} %copy-done.37, f32[128]{0:T(128)S(1)} %copy-done.38, ...), kind=kLoop, calls=%fused_computation.126 | loop fusion | flops 13078528 | bytes 24251392 | tf_op jit(solution)/shard_map/reduce_sum | solution.py:79
  464.0 11.8 %multiply_reduce_fusion.7 = (f32[4096]{0:T(1024)}, f32[4096]{0:T(1024)}, f32[4096]{0:T(1024)}, f32[4096]{0:T(1024)}, f32[4096]{0:T(1024)}, /*index=5*/f32[4096]{0:T(1024)}, f32[4096]{0:T(1024)}, f32[128,4096]{0,1:T(8,128)}) fusion(f32[134,4096]{0,1:T(8,128)S(1)} %copy-done, f32[128]{0:T(128)S(1)} %copy-done.37, f32[128]{0:T(128)S(1)} %copy-done.38, ...), kind=kLoop, calls=%fused_computation.133 | loop fusion | flops 13078528 | bytes 24251392 | tf_op jit(solution)/shard_map/reduce_sum | solution.py:79
  475.9 1.0 copy.71
  476.9 1.9 collective-permute-start.7
  478.9 1.0 copy.69
  480.0 1.9 collective-permute-start.6
  481.9 0.9 stack.109
  482.9 1.0 stack.100
  483.8 0.8 pad_maximum_fusion.4
  484.7 5.0 collective-permute-done.6
  489.7 1.8 copy.70
  491.5 14.3 %fusion.80 = bf16[1,128,4096]{1,2,0:T(8,128)(2,1)S(1)} fusion(f32[128]{0:T(128)S(1)} %copy-done.45, f32[6,4096]{0,1:T(8,128)} %copy.70, f32[128,4096]{0,1:T(8,128)S(1)} %copy-done.4, f32[4096]{0:T(1024)S(1)} %bitcast.145, f32[128]{0:T(128)S(1)} %copy-done.47, f32[4096]{0:T(1024)S(1)} %bitcast.147, f32[128]{0:T(128)S(1)} %copy-done.49, ...), kind=kLoop, calls=%fused_computation.154 | loop fusion | flops 13631488 | bytes 3361792 | tf_op jit(solution)/shard_map/broadcast_in_dim | solution.py:201
  505.8 2.8 copy.72
  508.6 15.0 %fusion.81 = bf16[1,128,4096]{1,2,0:T(8,128)(2,1)} fusion(f32[128]{0:T(128)S(1)} %copy-done.45, f32[6,4096]{0,1:T(8,128)} %copy.72, f32[128,4096]{0,1:T(8,128)S(1)} %copy-done.3, f32[4096]{0:T(1024)S(1)} %bitcast.175, f32[128]{0:T(128)S(1)} %copy-done.47, f32[4096]{0:T(1024)S(1)} %bitcast.173, f32[128]{0:T(128)S(1)} %copy-done.49, f32[4096]{0:T(1024)S(1)} %bitcast.135, ...), kind=kLoop, calls=%fused_computation.155 | loop fusion | flops 13631488 | bytes 3361792 | tf_op jit(solution)/shard_map/broadcast_in_dim | solution.py:202
  523.6 1.3 copy.76
  524.9 1.3 copy.77
  526.2 211.5 %all-reduce.4.cloned.1.call-done = (f32[3,7,4096]{2,1,0:T(8,128)}, f32[256,128]{0,1:T(8,128)}) async-done(((f32[3,7,4096]{2,1,0:T(8,128)}, f32[256,128]{0,1:T(8,128)}), (f32[3,7,4096]{2,1,0:T(8,128)}, f32[256,128]{0,1:T(8,128)})) %all-reduce.4.cloned.1.call-update) | async-done | bytes 475152 | tf_op jit(solution)/shard_map/psum | solution.py:194
  737.8 1.8 broadcast_multiply_fusion.2
  739.6 0.9 broadcast_multiply_fusion.3
  (147 shorter events, 7.7 us)
Async XLA Ops:
  7.2 28.5 %copy-start.8 = (bf16[1,128,4096]{2,1,0:T(8,128)(2,1)S(1)}, bf16[1,128,4096]{2,1,0:T(8,128)(2,1)}, u32[]{:S(2)}) copy-start(bf16[1,128,4096]{2,1,0:T(8,128)(2,1)} %param.8) | copy-start | bytes 3145732
  7.2 29.1 %copy-start.9 = (bf16[1,128,4096]{2,1,0:T(8,128)(2,1)S(1)}, bf16[1,128,4096]{2,1,0:T(8,128)(2,1)}, u32[]{:S(2)}) copy-start(bf16[1,128,4096]{2,1,0:T(8,128)(2,1)} %param.9) | copy-start | bytes 3145732
  7.2 730.6 %all-reduce.4.cloned.1.call-start = ((), (), s32[]{:S(2)}) async-start(), calls=%async_computation | async-start | bytes 1048576 | tf_op jit(solution)/shard_map/psum | solution.py:194
  8.9 94.4 %collective-permute-start.2 = (bf16[6,4096]{1,0:T(8,128)(2,1)}, bf16[6,4096]{1,0:T(8,128)(2,1)}, u32[]{:S(2)}, u32[]{:S(2)}) collective-permute-start(bf16[6,4096]{1,0:T(8,128)(2,1)} %slice_bitcast_fusion), channel_id=1, source_target_pairs={{0,16},{16,32},{32,48},{48,64},{64,80},{80,96},{96,112},{112,128},... | collective-permute-start | bytes 147464 | tf_op jit(solution)/shard_map/ppermute | solution.py:12
  20.6 89.0 %collective-permute-start.1 = (bf16[6,4096]{1,0:T(8,128)(2,1)}, bf16[6,4096]{1,0:T(8,128)(2,1)}, u32[]{:S(2)}, u32[]{:S(2)}) collective-permute-start(bf16[6,4096]{1,0:T(8,128)(2,1)} %slice_bitcast_fusion.1), channel_id=1, source_target_pairs={{0,16},{16,32},{32,48},{48,64},{64,80},{80,96},{96,112},{112,128},... | collective-permute-start | bytes 147464 | tf_op jit(solution)/shard_map/ppermute | solution.py:12
  24.0 89.6 %collective-permute-start = (bf16[6,4096]{1,0:T(8,128)(2,1)}, bf16[6,4096]{1,0:T(8,128)(2,1)}, u32[]{:S(2)}, u32[]{:S(2)}) collective-permute-start(bf16[6,4096]{1,0:T(8,128)(2,1)} %slice_bitcast_fusion.2), channel_id=1, source_target_pairs={{0,16},{16,32},{32,48},{48,64},{64,80},{80,96},{96,112},{112,128},... | collective-permute-start | bytes 147464 | tf_op jit(solution)/shard_map/ppermute | solution.py:12
  35.7 231.2 %copy-start.35 = (f32[128]{0:T(128)}, f32[128]{0:T(128)S(1)}, u32[]{:S(2)}) copy-start(f32[128]{0:T(128)S(1)} %get-tuple-element.82) | copy-start | bytes 1540
  114.9 3.0 copy-start.12
  115.0 3.0 copy-start.13
  115.0 3.0 copy-start.14
  115.0 2.9 copy-start.15
  115.0 2.9 copy-start.16
  115.0 2.9 copy-start.17
  115.0 2.9 copy-start.18
  115.0 2.9 copy-start.19
  115.0 2.9 copy-start.20
  115.0 2.9 copy-start.21
  115.0 2.9 copy-start.22
  115.1 2.9 copy-start.23
  115.1 2.9 copy-start.24
  115.1 2.9 copy-start.25
  115.1 2.9 copy-start.26
  115.1 2.9 copy-start.27
  115.1 2.9 copy-start.28
  115.1 2.9 copy-start.29
  115.1 2.9 copy-start.30
  115.1 2.9 copy-start.31
  115.1 2.9 copy-start.33
  115.2 2.9 copy-start.37
  115.2 2.9 copy-start.38
  115.2 2.9 copy-start.39
  115.2 2.9 copy-start.40
  115.2 2.9 copy-start.41
  154.9 96.6 %collective-permute-start.3 = (bf16[128,4096]{0,1:T(8,128)(2,1)}, bf16[128,4096]{0,1:T(8,128)(2,1)}, u32[]{:S(2)}, u32[]{:S(2)}) collective-permute-start(bf16[128,4096]{0,1:T(8,128)(2,1)} %get-tuple-element.52), channel_id=1, source_target_pairs={{0,16},{16,32},{32,48},{48,64},{64,80},{80,96},{96,112},{112,128},... | collective-permute-start | bytes 3145736 | tf_op jit(solution)/shard_map/ppermute | solution.py:12
  156.8 14.2 %copy-start.54 = (s32[128]{0:T(128)S(1)}, s32[128]{0:T(128)}, u32[]{:S(2)}) copy-start(s32[128]{0:T(128)} %get-tuple-element.90) | copy-start | bytes 1540
  171.0 252.1 %copy-start.42 = (f32[128]{0:T(128)}, f32[128]{0:T(128)S(1)}, u32[]{:S(2)}) copy-start(f32[128]{0:T(128)S(1)} %get-tuple-element.92) | copy-start | bytes 1540
  171.0 252.1 %copy-start.44 = (f32[128]{0:T(128)}, f32[128]{0:T(128)S(1)}, u32[]{:S(2)}) copy-start(f32[128]{0:T(128)S(1)} %get-tuple-element.93) | copy-start | bytes 1540
  171.0 252.1 %copy-start.46 = (f32[128]{0:T(128)}, f32[128]{0:T(128)S(1)}, u32[]{:S(2)}) copy-start(f32[128]{0:T(128)S(1)} %get-tuple-element.94) | copy-start | bytes 1540
  171.0 252.1 %copy-start.48 = (f32[128]{0:T(128)}, f32[128]{0:T(128)S(1)}, u32[]{:S(2)}) copy-start(f32[128]{0:T(128)S(1)} %get-tuple-element.95) | copy-start | bytes 1540
  171.0 252.1 %copy-start.50 = (f32[128]{0:T(128)}, f32[128]{0:T(128)S(1)}, u32[]{:S(2)}) copy-start(f32[128]{0:T(128)S(1)} %get-tuple-element.96) | copy-start | bytes 1540
  171.0 252.1 %copy-start.52 = (f32[128]{0:T(128)}, f32[128]{0:T(128)S(1)}, u32[]{:S(2)}) copy-start(f32[128]{0:T(128)S(1)} %get-tuple-element.97) | copy-start | bytes 1540
  254.7 12.2 %copy-start.11 = (f32[4096]{0:T(1024)S(1)}, f32[4096]{0:T(1024)}, u32[]{:S(2)}) copy-start(f32[4096]{0:T(1024)} %param.13) | copy-start | bytes 49156
  286.7 1.3 copy-start.5
  286.7 9.0 %copy-start.10 = (f32[128,256]{1,0:T(8,128)S(1)}, f32[128,256]{1,0:T(8,128)}, u32[]{:S(2)}) copy-start(f32[128,256]{1,0:T(8,128)} %get-tuple-element.88) | copy-start | bytes 393220
  290.7 130.7 %collective-permute-start.4 = (bf16[6,4096]{1,0:T(8,128)(2,1)S(1)}, bf16[6,4096]{1,0:T(8,128)(2,1)S(1)}, u32[]{:S(2)}, u32[]{:S(2)}) collective-permute-start(bf16[6,4096]{1,0:T(8,128)(2,1)S(1)} %copy.66), channel_id=1, source_target_pairs={{16,0},{32,16},{48,32},{64,48},{80,64},{96,80},{112,96},{128,112},... | collective-permute-start | bytes 147464 | tf_op jit(solution)/shard_map/ppermute | solution.py:12
  293.3 151.0 %collective-permute-start.5 = (bf16[128,4096]{0,1:T(8,128)(2,1)}, bf16[128,4096]{0,1:T(8,128)(2,1)}, u32[]{:S(2)}, u32[]{:S(2)}) collective-permute-start(bf16[128,4096]{0,1:T(8,128)(2,1)} %get-tuple-element.60), channel_id=1, source_target_pairs={{16,0},{32,16},{48,32},{64,48},{80,64},{96,80},{112,96},{128,112},... | collective-permute-start | bytes 3145736 | tf_op jit(solution)/shard_map/ppermute | solution.py:12
  295.8 17.6 %copy-start.6 = (bf16[128,4096]{0,1:T(8,128)(2,1)S(1)}, bf16[128,4096]{0,1:T(8,128)(2,1)}, u32[]{:S(2)}) copy-start(bf16[128,4096]{0,1:T(8,128)(2,1)} %get-tuple-element.60) | copy-start | bytes 3145732
  444.3 8.1 %copy-start.1 = (f32[134,4096]{0,1:T(8,128)S(1)}, f32[134,4096]{0,1:T(8,128)}, u32[]{:S(2)}) copy-start(f32[134,4096]{0,1:T(8,128)} %maximum_convert_fusion.2) | copy-start | bytes 6586372
  444.3 8.1 %copy-start.36 = (f32[128]{0:T(128)S(1)}, f32[128]{0:T(128)}, u32[]{:S(2)}) copy-start(f32[128]{0:T(128)} %copy-done.35) | copy-start | bytes 1540
  452.4 11.6 %copy-start = (f32[134,4096]{0,1:T(8,128)S(1)}, f32[134,4096]{0,1:T(8,128)}, u32[]{:S(2)}) copy-start(f32[134,4096]{0,1:T(8,128)} %maximum_convert_fusion.1) | copy-start | bytes 6586372
  464.0 11.8 %copy-start.2 = (f32[128,4096]{0,1:T(8,128)S(1)}, f32[128,4096]{0,1:T(8,128)}, u32[]{:S(2)}) copy-start(f32[128,4096]{0,1:T(8,128)} %get-tuple-element.58) | copy-start | bytes 6291460
  475.8 3.1 copy-start.4
  476.9 28.9 %collective-permute-start.7 = (bf16[6,4096]{1,0:T(8,128)(2,1)}, bf16[6,4096]{1,0:T(8,128)(2,1)}, u32[]{:S(2)}, u32[]{:S(2)}) collective-permute-start(bf16[6,4096]{1,0:T(8,128)(2,1)} %copy.71), channel_id=1, source_target_pairs={{16,0},{32,16},{48,32},{64,48},{80,64},{96,80},{112,96},{128,112},... | collective-permute-start | bytes 147464 | tf_op jit(solution)/shard_map/ppermute | solution.py:12
  480.0 9.7 %collective-permute-start.6 = (bf16[6,4096]{1,0:T(8,128)(2,1)}, bf16[6,4096]{1,0:T(8,128)(2,1)S(1)}, u32[]{:S(2)}, u32[]{:S(2)}) collective-permute-start(bf16[6,4096]{1,0:T(8,128)(2,1)} %copy.69), channel_id=1, source_target_pairs={{16,0},{32,16},{48,32},{64,48},{80,64},{96,80},{112,96},{128,112},... | collective-permute-start | bytes 147464 | tf_op jit(solution)/shard_map/ppermute | solution.py:12
  482.8 8.7 %copy-start.43 = (f32[128]{0:T(128)S(1)}, f32[128]{0:T(128)}, u32[]{:S(2)}) copy-start(f32[128]{0:T(128)} %copy-done.42) | copy-start | bytes 1540
  482.8 8.6 %copy-start.45 = (f32[128]{0:T(128)S(1)}, f32[128]{0:T(128)}, u32[]{:S(2)}) copy-start(f32[128]{0:T(128)} %copy-done.44) | copy-start | bytes 1540
  482.8 8.6 %copy-start.47 = (f32[128]{0:T(128)S(1)}, f32[128]{0:T(128)}, u32[]{:S(2)}) copy-start(f32[128]{0:T(128)} %copy-done.46) | copy-start | bytes 1540
  482.8 8.6 %copy-start.49 = (f32[128]{0:T(128)S(1)}, f32[128]{0:T(128)}, u32[]{:S(2)}) copy-start(f32[128]{0:T(128)} %copy-done.48) | copy-start | bytes 1540
  482.8 8.6 %copy-start.51 = (f32[128]{0:T(128)S(1)}, f32[128]{0:T(128)}, u32[]{:S(2)}) copy-start(f32[128]{0:T(128)} %copy-done.50) | copy-start | bytes 1540
  482.8 8.6 %copy-start.53 = (f32[128]{0:T(128)S(1)}, f32[128]{0:T(128)}, u32[]{:S(2)}) copy-start(f32[128]{0:T(128)} %copy-done.52) | copy-start | bytes 1540
  505.8 2.8 copy-start.3
  505.8 2.8 copy-start.32
  505.8 2.8 copy-start.34
  523.6 1.3 copy-start.7
Sparse Core Ops, SparseCore 0:
  484.8 252.9 all-reduce.3
where the time goes:
time: 759 us; the launch traced here: 748 us
  waiting for transfers between devices  217 us (29%)
  local copies, waits for them, and re-layouts  192 us (25%)
  other arithmetic  175 us (23%)
  blocking collectives  79.8 us (11%)
  matrix products  44.9 us (6%)
  starting transfers between devices  24.8 us (3%)
  between operations  15.1 us (2%)
    psum x1, waiting for transfers between devices, shards(): lax.psum((short_local, filter_local, skip_local), ('ctx', 'dp'))  212 us
    psum x1, blocking collectives, shards(): lax.psum((short_local, filter_local, skip_local), ('ctx', 'dp'))  79.8 us
    reduce_sum x3, other arithmetic, tap_grads(): jnp.sum(gradient * extended[margin - offset:margin - offset + number] * m...  43.2 us
    reduce_sum x1, other arithmetic, shards(): skip_local = jnp.sum(dz * u_float, axis=0)  36.8 us
    reshape x1, local copies, waits for them, and re-layouts, diagonal_sums(): flat = dmat.reshape(groups, length * double)  35 us
    reshape x1, local copies, waits for them, and re-layouts, diagonal_sums(): folded = jnp.sum(flat.reshape(groups, length, double + 1), axis=1)  28.3 us
    another operation x2, local copies, waits for them, and re-layouts, toeplitz(): tiled = jnp.tile(pattern, (1, length))[:, :2 * length * length]  25.4 us
    ppermute x8, starting transfers between devices, from_behind(): lax.ppermute(value, axis, [(source, source + steps) for source in range(l...  24.8 us
  transfers between devices with their start and end apart: 9, of which 2 were waited for; matrix products, arithmetic and copies ran while one was open for 39% of the time, Pallas kernels for 0%

commit v1 on v0

v1 whole, which is shorter than its diff:
```python
import functools
import math

import jax
import jax.numpy as jnp
from jax import lax
from jax.experimental import pallas as pl
from jax.experimental.pallas import tpu as pltpu
from jax.sharding import PartitionSpec as P

MESH = pl.DeviceIdType.MESH
LANES = 128
HALO = 8
AHEAD = 2


def device(ctx, dp):
    return {"ctx": ctx, "dp": dp}


def block_kernel(
    steps,
    group_width,
    lengths,
    query,
    keys,
    values,
    cotangent,
    taps,
    filters,
    flipped,
    skip,
    mixed,
    grad_query,
    grad_key,
    grad_value,
    partial,
    window,
    feats,
    u_own,
    dz_own,
    u_prior,
    dz_next,
    head_out,
    head_in,
    back_out,
    back_in,
    feat_mask,
    back_mask,
    conv_mask,
    conv_keep,
    du_mask,
    grads,
    tails,
    sums,
    send_u,
    recv_u,
    send_dz,
    recv_dz,
    send_head,
    recv_head,
    send_back,
    recv_back,
):
    me = lax.axis_index("ctx")
    row = lax.axis_index("dp")
    count = lax.axis_size("ctx")
    after, before = lax.rem(me + 1, count), lax.rem(me + count - 1, count)
    tokens = query.shape[0]
    chunk = u_own.shape[2]
    tiles = chunk // LANES
    count_taps = taps.shape[1]
    per_tile = LANES // group_width
    has_prior, has_next = me > 0, me < count - 1
    streams = (query, keys, values)
    outputs = (grad_query, grad_key, grad_value)

    def head_copy(n):
        return pltpu.make_async_remote_copy(
            src_ref=head_out.at[n],
            dst_ref=head_in.at[n],
            send_sem=send_head.at[n],
            recv_sem=recv_head.at[n],
            device_id=device(after, row),
            device_id_type=MESH,
        )

    def u_copy(n):
        return pltpu.make_async_remote_copy(
            src_ref=u_own.at[n],
            dst_ref=u_prior.at[n],
            send_sem=send_u.at[n],
            recv_sem=recv_u.at[n],
            device_id=device(after, row),
            device_id_type=MESH,
        )

    def dz_copy(n):
        return pltpu.make_async_remote_copy(
            src_ref=dz_own.at[n],
            dst_ref=dz_next.at[n],
            send_sem=send_dz.at[n],
            recv_sem=recv_dz.at[n],
            device_id=device(before, row),
            device_id_type=MESH,
        )

    def back_copy(n):
        return pltpu.make_async_remote_copy(
            src_ref=back_out.at[n],
            dst_ref=back_in.at[n],
            send_sem=send_back.at[n],
            recv_sem=recv_back.at[n],
            device_id=device(before, row),
            device_id_type=MESH,
        )

    barrier = pltpu.get_barrier_semaphore()
    for neighbour in (after, before):
        pl.semaphore_signal(
            barrier, inc=1, device_id=device(neighbour, row), device_id_type=MESH
        )

    def stage_head(n, carry):
        lanes = pl.ds(pl.multiple_of(n * chunk, chunk), chunk)
        last = [
            ref[tokens - 16 : tokens, lanes].astype(jnp.float32)[16 - HALO :] for ref in streams
        ]
        blank = jnp.zeros((HALO, chunk), jnp.float32)
        head_out[n] = jnp.concatenate(last + [blank], 0).astype(jnp.bfloat16)
        back_out[n] = jnp.zeros(back_out.shape[1:], jnp.bfloat16)
        return carry

    lax.fori_loop(0, steps, stage_head, 0)

    @pl.when(jnp.logical_not(has_prior))
    def _():
        u_prior[...] = jnp.zeros(u_prior.shape, u_prior.dtype)
        head_in[...] = jnp.zeros(head_in.shape, head_in.dtype)

    @pl.when(jnp.logical_not(has_next))
    def _():
        dz_next[...] = jnp.zeros(dz_next.shape, dz_next.dtype)
        back_in[...] = jnp.zeros(back_in.shape, back_in.dtype)

    pl.semaphore_wait(barrier, 2)

    @pl.when(has_next)
    def _():
        def send_heads(n, carry):
            head_copy(n).start()
            return carry

        lax.fori_loop(0, steps, send_heads, 0)

    starts = [jnp.int32(0)]
    for index in range(lengths.shape[1] - 1):
        starts.append(starts[-1] + lengths[0, index])

    def docs(positions):
        result = jnp.full(positions.shape, -1, jnp.int32)
        for start in starts:
            result = result + (positions >= start).astype(jnp.int32)
        return result

    def iota(shape, dim):
        return lax.broadcasted_iota(jnp.int32, shape, dim)

    anchor = me * tokens
    wide = (tokens, 2 * tokens)
    target, source = iota(wide, 0), iota(wide, 1) - tokens
    lag = target - source
    own_docs = docs(iota((tokens, LANES), 0) + anchor)
    same = jnp.concatenate([own_docs] * (2 * tokens // LANES), 1) == docs(source + anchor)
    conv_mask[...] = jnp.where(same & (lag >= 0) & (lag < tokens), 1.0, 0.0).astype(jnp.bfloat16)
    target = tokens - 1 - target
    lag = target - source
    same = docs(target + anchor) == docs(source + anchor)
    conv_keep[...] = jnp.where(same & (lag >= 0) & (lag < tokens), 1.0, 0.0)
    lag = iota(wide, 1) - iota(wide, 0)
    same = jnp.concatenate([own_docs] * (2 * tokens // LANES), 1) == docs(iota(wide, 1) + anchor)
    du_mask[...] = jnp.where(same & (lag >= 0) & (lag < tokens), 1.0, 0.0).astype(jnp.bfloat16)
    spread = (tokens + HALO, LANES)
    here = iota(spread, 0) - HALO
    here_docs = docs(here + anchor)
    for offset in range(count_taps):
        if offset:
            prior_docs = docs(iota((tokens, LANES), 0) + (anchor - offset))
            feat_mask[offset - 1] = jnp.where(prior_docs == own_docs, 1.0, 0.0)
        there = here + offset
        fits = (there >= 0) & (there < tokens) & (docs(there + anchor) == here_docs)
        back_mask[offset] = jnp.where(fits, 1.0, 0.0)
    for stream in range(3):
        grads[stream, 0:HALO] = jnp.zeros((HALO, LANES), jnp.float32)
        grads[stream, HALO + tokens :] = jnp.zeros((HALO, LANES), jnp.float32)
    sums[...] = jnp.zeros(sums.shape, jnp.float32)
    lane_group = iota((tokens, LANES), 1) // group_width
    opposite = iota((tokens, LANES), 0) + iota((tokens, LANES), 1) == tokens - 1
    upside = jnp.where(opposite, 1.0, 0.0).astype(jnp.bfloat16)

    def featurize(n, i):
        tile = n * tiles + i
        lanes = pl.ds(pl.multiple_of(tile * LANES, LANES), LANES)
        inner = pl.ds(pl.multiple_of(i * LANES, LANES), LANES)
        first = head_in[n, 0:16, inner].astype(jnp.float32)
        second = head_in[n, 16:32, inner].astype(jnp.float32)
        heads = (first[:HALO], first[HALO:], second[:HALO])
        made = []
        for stream in range(3):
            window[tile, stream, 0:HALO] = heads[stream]
            own = streams[stream][:, lanes].astype(jnp.float32)
            window[tile, stream, HALO : HALO + tokens] = own
            result = taps[stream, 0:1, lanes] * own
            for offset in range(1, count_taps):
                shifted = window[tile, stream, HALO - offset : HALO - offset + tokens]
                result = result + taps[stream, offset : offset + 1, lanes] * (
                    shifted * feat_mask[offset - 1]
                )
            feats[tile, stream] = result
            made.append(result)
        u_own[n, :, inner] = (made[1] * made[2]).astype(jnp.bfloat16)
        gradient = cotangent[:, lanes].astype(jnp.float32)
        dz_own[n, :, inner] = (gradient * made[0]).astype(jnp.bfloat16)

    def convolve(n, i):
        tile = n * tiles + i
        lanes = pl.ds(pl.multiple_of(tile * LANES, LANES), LANES)
        inner = pl.ds(pl.multiple_of(i * LANES, LANES), LANES)
        u_tile = u_own[n, :, inner]
        dz_tile = dz_own[n, :, inner]
        dz_turned = jnp.dot(upside, dz_tile, preferred_element_type=jnp.float32)
        dz_turned = dz_turned.astype(jnp.bfloat16)
        u_window = jnp.concatenate([u_prior[n, :, inner], u_tile], 0)
        dz_window = jnp.concatenate([dz_tile, dz_next[n, :, inner]], 0)
        conv = jnp.zeros((tokens, LANES), jnp.float32)
        du = jnp.zeros((tokens, LANES), jnp.float32)
        rows = pl.ds(pl.multiple_of(tile * per_tile, per_tile), per_tile)
        own_taps, own_flipped = filters[rows], flipped[rows]
        for group in range(per_tile):
            mine = lane_group == group

            def circulant(line):
                spread_line = jnp.broadcast_to(line[group : group + 1], (tokens, LANES))
                turned = pltpu.roll(spread_line, 0, 1, stride=1, stride_axis=0)
                half = turned.astype(jnp.bfloat16)
                return jnp.concatenate([half, half], 1)

            piece = jnp.dot(
                circulant(own_flipped) * conv_mask[...],
                u_window,
                preferred_element_type=jnp.float32,
            )
            conv = jnp.where(mine, piece, conv)
            piece = jnp.dot(
                circulant(own_taps) * du_mask[...],
                dz_window,
                preferred_element_type=jnp.float32,
            )
            du = jnp.where(mine, piece, du)
            chosen = jnp.where(mine, dz_turned, jnp.zeros_like(dz_turned))
            outer = lax.dot_general(
                chosen,
                u_window,
                (((1,), (1,)), ((), ())),
                preferred_element_type=jnp.float32,
            )
            outer = outer * conv_keep[...]
            folded = outer[:, :LANES] + outer[:, LANES:]
            turned = pltpu.roll(folded, 0, 1, stride=1, stride_axis=0)
            sums[24 + group : 25 + group] = jnp.sum(turned, axis=0, keepdims=True)
        u_float = u_tile.astype(jnp.float32)
        gradient = cotangent[:, lanes].astype(jnp.float32)
        gain = skip[:, lanes]
        q_feat = feats[tile, 0]
        dz = gradient * q_feat
        total = conv + gain * u_float
        mixed[:, lanes] = (q_feat * total).astype(jnp.bfloat16)
        sums[3 * count_taps : 3 * count_taps + 1] = jnp.sum(dz * u_float, axis=0, keepdims=True)
        du = du + gain * dz
        inside = pl.ds(HALO, tokens)
        grads[0, inside] = gradient * total
        grads[1, inside] = du * feats[tile, 2]
        grads[2, inside] = du * feats[tile, 1]
        heads = []
        for stream in range(3):
            result = None
            x_window = window[tile, stream]
            for offset in range(count_taps):
                shifted = grads[stream, offset : offset + tokens + HALO] * back_mask[offset]
                term = taps[stream, offset : offset + 1, lanes] * shifted
                result = term if result is None else result + term
                line = stream * count_taps + offset
                sums[line : line + 1] = jnp.sum(shifted * x_window, axis=0, keepdims=True)
            heads.append(result[:HALO])
            tails[stream, :, lanes] = result[HALO + tokens - 16 :]
            outputs[stream][:, lanes] = result[HALO:].astype(jnp.bfloat16)
        heads.append(jnp.zeros((HALO, LANES), jnp.float32))
        back_out[n, :, inner] = jnp.concatenate(heads, 0).astype(jnp.bfloat16)
        partial[tile] = sums[...].astype(jnp.bfloat16)

    def step(n, carry):
        @pl.when(n < steps)
        def _():
            @pl.when(has_prior)
            def _():
                head_copy(n).wait_recv()

            def one(i, inside):
                featurize(n, i)
                return inside

            lax.fori_loop(0, tiles, one, 0)

            @pl.when(has_next)
            def _():
                u_copy(n).start()

            @pl.when(has_prior)
            def _():
                dz_copy(n).start()

        @pl.when(n >= AHEAD)
        def _():
            past = n - AHEAD

            @pl.when(has_prior)
            def _():
                u_copy(past).wait_recv()

            @pl.when(has_next)
            def _():
                dz_copy(past).wait_recv()

            def one(i, inside):
                convolve(past, i)
                return inside

            lax.fori_loop(0, tiles, one, 0)

            @pl.when(has_prior)
            def _():
                back_copy(past).start()

        return carry

    lax.fori_loop(0, steps + AHEAD, step, 0)

    def finish(n, carry):
        @pl.when(has_next)
        def _():
            back_copy(n).wait_recv()

        lanes = pl.ds(pl.multiple_of(n * chunk, chunk), chunk)
        first = back_in[n, 0:16].astype(jnp.float32)
        second = back_in[n, 16:32].astype(jnp.float32)
        arrived = (first[:HALO], first[HALO:], second[:HALO])
        for stream in range(3):
            tail = tails[stream, :, lanes]
            fixed = jnp.concatenate([tail[:HALO], tail[HALO:] + arrived[stream]], 0)
            outputs[stream][tokens - 16 : tokens, lanes] = fixed.astype(jnp.bfloat16)

        @pl.when(has_next)
        def _():
            head_copy(n).wait_send()
            u_copy(n).wait_send()

        @pl.when(has_prior)
        def _():
            dz_copy(n).wait_send()
            back_copy(n).wait_send()

        return carry

    lax.fori_loop(0, steps, finish, 0)


def local_block(steps, query, keys, values, cotangent, taps, filters, skip, lengths):
    tokens, width = query.shape
    groups, filter_len = filters.shape
    chunk = width // steps
    tiles = width // LANES
    count_taps = taps.shape[1]
    rounded = filters.astype(jnp.bfloat16).astype(jnp.float32)
    flipped = jnp.concatenate([rounded[:, :1], rounded[:, :0:-1]], 1)
    stream = jax.ShapeDtypeStruct((tokens, width), jnp.bfloat16)
    vmem = pl.BlockSpec(memory_space=pltpu.VMEM)
    dma = pltpu.SemaphoreType.DMA((steps,))
    piece = pltpu.VMEM((steps, tokens, chunk), jnp.bfloat16)
    margin = pltpu.VMEM((steps, 32, chunk), jnp.bfloat16)
    return pl.pallas_call(
        functools.partial(block_kernel, steps, width // groups),
        out_shape=[stream] * 4 + [jax.ShapeDtypeStruct((tiles, 32, LANES), jnp.bfloat16)],
        in_specs=[pl.BlockSpec(memory_space=pltpu.SMEM)] + [vmem] * 8,
        out_specs=[vmem] * 5,
        scratch_shapes=[
            pltpu.VMEM((tiles, 3, tokens + HALO, LANES), jnp.float32),
            pltpu.VMEM((tiles, 3, tokens, LANES), jnp.float32),
            piece,
            piece,
            piece,
            piece,
            margin,
            margin,
            margin,
            margin,
            pltpu.VMEM((count_taps - 1, tokens, LANES), jnp.float32),
            pltpu.VMEM((count_taps, tokens + HALO, LANES), jnp.float32),
            pltpu.VMEM((tokens, 2 * tokens), jnp.bfloat16),
            pltpu.VMEM((tokens, 2 * tokens), jnp.float32),
            pltpu.VMEM((tokens, 2 * tokens), jnp.bfloat16),
            pltpu.VMEM((3, tokens + 2 * HALO, LANES), jnp.float32),
            pltpu.VMEM((3, 16, width), jnp.float32),
            pltpu.VMEM((32, LANES), jnp.float32),
        ]
        + [dma] * 8,
        compiler_params=pltpu.CompilerParams(
            collective_id=0, has_side_effects=True, vmem_limit_bytes=56 * 2**20
        ),
        name="block",
    )(lengths, query, keys, values, cotangent, taps, rounded, flipped, skip)


def reduce_kernel(
    scale,
    partial,
    result,
    gathered,
    stacked,
    spread_sums,
    send_one,
    recv_one,
    send_two,
    recv_two,
    send_three,
    recv_three,
):
    ctx, dp = lax.axis_index("ctx"), lax.axis_index("dp")
    x, high, core = ctx // 4, lax.rem(ctx // 2, 2), lax.rem(ctx, 2)
    low, y = dp // 4, lax.rem(dp, 4)
    place = (x * 2 + core) * 4 + y
    depth = high * 4 + low
    planes = gathered.shape[0]
    depths = stacked.shape[0]

    def in_plane(index):
        return device(
            (index // 8) * 4 + high * 2 + lax.rem(index // 4, 2), low * 4 + lax.rem(index, 4)
        )

    def in_depth(index):
        return device(x * 4 + (index // 4) * 2 + core, lax.rem(index, 4) * 4 + y)

    def first(peer, slot):
        return pltpu.make_async_remote_copy(
            src_ref=partial.at[peer],
            dst_ref=gathered.at[slot],
            send_sem=send_one.at[peer],
            recv_sem=recv_one.at[slot],
            device_id=in_plane(peer),
            device_id_type=MESH,
        )

    def second(peer, slot):
        return pltpu.make_async_remote_copy(
            src_ref=stacked.at[depth],
            dst_ref=stacked.at[slot],
            send_sem=send_two.at[peer],
            recv_sem=recv_two.at[slot],
            device_id=in_depth(peer),
            device_id_type=MESH,
        )

    def third(peer, slot):
        return pltpu.make_async_remote_copy(
            src_ref=spread_sums.at[place],
            dst_ref=spread_sums.at[slot],
            send_sem=send_three.at[peer],
            recv_sem=recv_three.at[slot],
            device_id=in_plane(peer),
            device_id_type=MESH,
        )

    def each(count, mine, action):
        def body(k, carry):
            action(lax.rem(mine + k, count))
            return carry

        lax.fori_loop(1, count, body, 0)

    barrier = pltpu.get_barrier_semaphore()

    def greet(where):
        def action(peer):
            pl.semaphore_signal(barrier, inc=1, device_id=where(peer), device_id_type=MESH)

        return action

    each(planes, place, greet(in_plane))
    each(depths, depth, greet(in_depth))
    pl.semaphore_wait(barrier, planes + depths - 2)

    each(planes, place, lambda peer: first(peer, place).start())
    gathered[place] = partial[place]
    each(planes, place, lambda peer: first(peer, peer).wait_recv())
    total = gathered[0].astype(jnp.float32)
    for index in range(1, planes):
        total = total + gathered[index].astype(jnp.float32)
    stacked[depth] = total
    each(depths, depth, lambda peer: second(peer, depth).start())
    each(depths, depth, lambda peer: second(peer, peer).wait_recv())
    total = stacked[0]
    for index in range(1, depths):
        total = total + stacked[index]
    spread_sums[place] = (total * scale).astype(jnp.bfloat16)
    each(planes, place, lambda peer: third(peer, place).start())
    each(planes, place, lambda peer: third(peer, peer).wait_recv())
    result[...] = spread_sums[...]
    each(planes, place, lambda peer: first(peer, place).wait_send())
    each(depths, depth, lambda peer: second(peer, depth).wait_send())
    each(planes, place, lambda peer: third(peer, place).wait_send())


def reduced(partial, scale):
    planes, rows, lanes = partial.shape
    depths = 8
    vmem = pl.BlockSpec(memory_space=pltpu.VMEM)
    plane_sems = pltpu.SemaphoreType.DMA((planes,))
    depth_sems = pltpu.SemaphoreType.DMA((depths,))
    return pl.pallas_call(
        functools.partial(reduce_kernel, scale),
        out_shape=jax.ShapeDtypeStruct(partial.shape, jnp.bfloat16),
        in_specs=[vmem],
        out_specs=vmem,
        scratch_shapes=[
            pltpu.VMEM((planes, rows, lanes), jnp.bfloat16),
            pltpu.VMEM((depths, rows, lanes), jnp.float32),
            pltpu.VMEM((planes, rows, lanes), jnp.bfloat16),
            plane_sems,
            plane_sems,
            depth_sems,
            depth_sems,
            plane_sems,
            plane_sems,
        ],
        compiler_params=pltpu.CompilerParams(
            collective_id=1, has_side_effects=True, vmem_limit_bytes=16 * 2**20
        ),
        name="reduce",
    )(partial)


def shards(
    query_proj, key_proj, value_proj, short_taps, filter_taps, skip_gain, doc_lengths, out_grad
):
    tokens, width = query_proj.shape[1:]
    count_taps = short_taps.shape[1]
    mixed, grad_query, grad_key, grad_value, partial = local_block(
        8,
        query_proj[0],
        key_proj[0],
        value_proj[0],
        out_grad[0],
        short_taps,
        filter_taps,
        skip_gain[None],
        doc_lengths,
    )
    scale = 1.0 / math.sqrt(tokens * lax.axis_size("ctx") * lax.axis_size("dp"))
    sums = reduced(partial, scale).astype(jnp.float32)
    lines = 3 * count_taps
    short = sums[:, :lines].transpose(1, 0, 2).reshape(3, count_taps, width)
    gain = sums[:, lines].reshape(width)
    folded = sums[:, 24:].reshape(filter_taps.shape)
    filters = folded[:, ::-1]
    return (
        mixed[None],
        grad_query[None],
        grad_key[None],
        grad_value[None],
        short,
        filters,
        gain,
    )


def solution(mesh):
    return jax.shard_map(
        shards,
        mesh=mesh,
        in_specs=(
            P("dp", "ctx", None),
            P("dp", "ctx", None),
            P("dp", "ctx", None),
            P(),
            P(),
            P(),
            P("dp", None),
            P("dp", "ctx", None),
        ),
        out_specs=(
            P("dp", "ctx", None),
            P("dp", "ctx", None),
            P("dp", "ctx", None),
            P("dp", "ctx", None),
            P(),
            P(),
            P(),
        ),
        check_vma=False,
    )
```

time: 759 us -> 123 us (0.16); the launches traced: 748 us -> 123 us
  waiting for transfers between devices: 217 us -> 0 us
  local copies, waits for them, and re-layouts: 192 us -> 9.74 us
  other arithmetic: 175 us -> 1.73 us
  Pallas kernels: 0 us -> 110 us
  blocking collectives: 79.8 us -> 0 us
  matrix products: 44.9 us -> 0 us
  starting transfers between devices: 24.8 us -> 0 us
  between operations: 15.1 us -> 0.72 us
    psum x1 -> x0, waiting for transfers between devices: 212 us -> none  [shards(): lax.psum((short_local, filter_local, skip_local), ('ctx', 'dp'))]
    pallas_call x0 -> x2, Pallas kernels: none -> 110 us  [the longest x1 66.3 us: local_block(): pl.pallas_call(functools.partial(block_kernel, steps, width // groups), o...]
    reduce_sum x7 -> x0, other arithmetic: 92 us -> none  [the longest x3 43.2 us: tap_grads(): jnp.sum(gradient * extended[margin - offset:margin - offset + number] * m...]
    reshape x3 -> x2, local copies, waits for them, and re-layouts: 86.4 us -> 0.82 us  [the longest x1 0.8 us: shards(): short = sums[:, :lines].transpose(1, 0, 2).reshape(3, count_taps, width)]
    psum x1 -> x0, blocking collectives: 79.8 us -> none  [shards(): lax.psum((short_local, filter_local, skip_local), ('ctx', 'dp'))]
    broadcast_in_dim x3 -> x0, other arithmetic: 48.2 us -> none  [the longest x1 18.9 us: shards(): grad_query[None]]
    dot_general x4 -> x0, matrix products: 44.9 us -> none  [the longest x1 17.6 us: shards(): jnp.einsum('gft,gfj->gtj', dz_cols, u_cols, preferred_element_type=jnp.fl...]
    slice x16 -> x2, local copies, waits for them, and re-layouts: 28.7 us -> 0.71 us  [the longest x1 0.62 us: shards(): gain = sums[:, lines].reshape(width)]
  transfers between devices with their start and end apart: 9 -> 0, of which waited for: 2 -> 0; matrix products, arithmetic and copies ran while one was open for 39% -> 0% of each run, Pallas kernels for 0% -> 0%
where the time goes in v1:
time: 123 us
  Pallas kernels  110 us (89%)
  local copies, waits for them, and re-layouts  9.74 us (8%)
  other arithmetic  1.73 us (1%)
    pallas_call x1, Pallas kernels, local_block(): pl.pallas_call(functools.partial(block_kernel, steps, width // groups), o...  66.3 us
    pallas_call x1, Pallas kernels, reduced(): pl.pallas_call(functools.partial(reduce_kernel, scale), out_shape=jax.Sha...  44.2 us
    unnamed x16, local copies, waits for them, and re-layouts  7.09 us

profile of v1, /device:TPU:1, one launch (start us, length us, event | category | flops | bytes accessed | tf_op | source)
XLA Modules:
  0.0 122.6 jit_solution(14387650154272654254)
XLA Ops:
  0.6 0.9 convert_convert_fusion.filters
  1.5 0.0 copy-start.1
  1.6 0.1 slice.21
  1.7 0.2 rev.6
  1.8 0.4 copy-done.1
  2.2 0.8 pad_maximum_fusion.flipped
  3.0 66.3 %block.1 = (bf16[128,4096]{1,0:T(8,128)(2,1)}, bf16[128,4096]{1,0:T(8,128)(2,1)}, bf16[128,4096]{1,0:T(8,128)(2,1)}, bf16[128,4096]{1,0:T(8,128)(2,1)}, bf16[32,32,128]{2,1,0:T(8,128)(2,1)}) custom-call(s32[1,8]{1,0:T(1,128)} %lengths.1, bf16[128,4096]{1,0:T(8,128)(2,1)} %bitcast.16, bf16[128,4096]{1,0:T(8,128)(2,1)} %bitcast.17, ...), custom_call_target="tpu_custom_call" | custom-call | tf_op jit(solution)/shard_map/block/pallas_call | solution.py:390
  69.2 0.0 copy-start
  69.2 0.9 copy-done
  70.2 44.2 %reduce.1 = bf16[32,32,128]{2,1,0:T(8,128)(2,1)S(1)} custom-call(bf16[32,32,128]{2,1,0:T(8,128)(2,1)S(1)} %copy-done), custom_call_target="tpu_custom_call" | custom-call | tf_op jit(solution)/shard_map/reduce/pallas_call | solution.py:529
  114.4 0.1 convert_element_type.11
  114.5 0.0 copy-start.5
  114.5 0.1 copy.15
  114.6 0.8 reshape.20
  115.4 0.8 rev.7
  116.2 0.6 slice.24
  116.8 0.0 copy-done.5
  116.8 0.0 copy-start.4
  116.8 1.0 copy.20
  117.8 0.6 copy-done.4
  118.4 0.0 copy-start.3
  118.4 1.0 copy.21
  119.4 0.6 copy-done.3
  120.0 0.0 copy-start.2
  120.0 1.0 copy.22
  121.0 0.6 copy-done.2
  121.6 1.0 copy.23
  (2 shorter events, 0.1 us)
Async XLA Ops:
  1.5 0.7 copy-start.1
  69.2 1.0 copy-start
  114.5 2.4 %copy-start.5 = (bf16[128,4096]{1,0:T(8,128)(2,1)S(1)}, bf16[128,4096]{1,0:T(8,128)(2,1)}, u32[]{:S(2)}) copy-start(bf16[128,4096]{1,0:T(8,128)(2,1)} %get-tuple-element.12) | copy-start | bytes 3145732
  116.8 1.6 %copy-start.4 = (bf16[128,4096]{1,0:T(8,128)(2,1)S(1)}, bf16[128,4096]{1,0:T(8,128)(2,1)}, u32[]{:S(2)}) copy-start(bf16[128,4096]{1,0:T(8,128)(2,1)} %get-tuple-element.13) | copy-start | bytes 3145732
  118.4 1.6 %copy-start.3 = (bf16[128,4096]{1,0:T(8,128)(2,1)S(1)}, bf16[128,4096]{1,0:T(8,128)(2,1)}, u32[]{:S(2)}) copy-start(bf16[128,4096]{1,0:T(8,128)(2,1)} %get-tuple-element.14) | copy-start | bytes 3145732
  120.0 1.6 %copy-start.2 = (bf16[128,4096]{1,0:T(8,128)(2,1)S(1)}, bf16[128,4096]{1,0:T(8,128)(2,1)}, u32[]{:S(2)}) copy-start(bf16[128,4096]{1,0:T(8,128)(2,1)} %get-tuple-element.15) | copy-start | bytes 3145732

commit v2 on v1

v2 whole, which is shorter than its diff:
```python
import functools
import math

import jax
import jax.numpy as jnp
from jax import lax
from jax.experimental import pallas as pl
from jax.experimental.pallas import tpu as pltpu
from jax.sharding import PartitionSpec as P

MESH = pl.DeviceIdType.MESH
LANES = 128
HALO = 8
STEPS = 8
AHEAD = 3
LEAD = 2
EARLY = 2
EDGE = 16
REFINE = 1


def device(ctx, dp):
    return {"ctx": ctx, "dp": dp}


def block_kernel(
    steps,
    group_width,
    scale,
    lengths,
    query,
    keys,
    values,
    cotangent,
    taps,
    filters,
    skip,
    mixed,
    grad_query,
    grad_key,
    grad_value,
    spread_sums,
    inputs,
    results,
    tails,
    window,
    feats,
    flipped,
    u_own,
    dz_own,
    u_prior,
    dz_next,
    head_out,
    head_in,
    back_out,
    back_in,
    heads,
    packed,
    places,
    feat_mask,
    back_mask,
    conv_mask,
    conv_keep,
    du_mask,
    grads,
    sums,
    partial,
    gathered,
    stacked,
    load_sem,
    store_sem,
    tail_sem,
    send_u,
    recv_u,
    send_dz,
    recv_dz,
    send_head,
    recv_head,
    send_back,
    recv_back,
    send_one,
    recv_one,
    send_two,
    recv_two,
    send_three,
    recv_three,
):
    me = lax.axis_index("ctx")
    row = lax.axis_index("dp")
    count = lax.axis_size("ctx")
    after, before = lax.rem(me + 1, count), lax.rem(me + count - 1, count)
    tokens, width = query.shape
    chunk = width // steps
    tiles = chunk // LANES
    count_taps = taps.shape[1]
    margin = count_taps - 1
    per_tile = LANES // group_width
    has_prior, has_next = me > 0, me < count - 1
    sources = (query, keys, values, cotangent)
    outputs = (mixed, grad_query, grad_key, grad_value)

    x, high, core = me // 4, lax.rem(me // 2, 2), lax.rem(me, 2)
    low, y = row // 4, lax.rem(row, 4)
    place = (x * 2 + core) * 4 + y
    depth = high * 4 + low
    planes = gathered.shape[0]
    depths = stacked.shape[0]
    owned = place // tiles

    def in_plane(index):
        return device(
            (index // 8) * 4 + high * 2 + lax.rem(index // 4, 2), low * 4 + lax.rem(index, 4)
        )

    def in_depth(index):
        return device(x * 4 + (index // 4) * 2 + core, lax.rem(index, 4) * 4 + y)

    def remote(source, target, send, recv, where):
        return pltpu.make_async_remote_copy(
            src_ref=source,
            dst_ref=target,
            send_sem=send,
            recv_sem=recv,
            device_id=where,
            device_id_type=MESH,
        )

    def head_copy(n):
        return remote(
            head_out.at[n], head_in.at[n], send_head.at[n], recv_head.at[n], device(after, row)
        )

    parts = (pl.ds(EDGE, tokens - EDGE), pl.ds(0, EDGE))

    def u_copy(n, part):
        rows = parts[part]
        return remote(
            u_own.at[n, rows], u_prior.at[n, rows], send_u.at[n, part], recv_u.at[n, part],
            device(after, row),
        )

    def dz_copy(n, part):
        rows = parts[part]
        return remote(
            dz_own.at[n, rows], dz_next.at[n, rows], send_dz.at[n, part], recv_dz.at[n, part],
            device(before, row),
        )

    def send_part(n, part):
        @pl.when(has_next)
        def _():
            u_copy(n, part).start()

        @pl.when(has_prior)
        def _():
            dz_copy(n, part).start()

    def back_copy(n):
        return remote(
            back_out.at[n], back_in.at[n], send_back.at[n], recv_back.at[n], device(before, row)
        )

    def first(peer, slot):
        return remote(
            partial.at[peer], gathered.at[slot], send_one.at[peer], recv_one.at[slot],
            in_plane(peer),
        )

    def second(peer, slot):
        return remote(
            stacked.at[depth], stacked.at[slot], send_two.at[peer], recv_two.at[slot],
            in_depth(peer),
        )

    def third(peer, slot):
        return remote(
            spread_sums.at[place], spread_sums.at[slot], send_three.at[peer],
            recv_three.at[slot], in_plane(peer),
        )

    def load(n, which):
        lanes = pl.ds(pl.multiple_of(n * chunk, chunk), chunk)
        return pltpu.make_async_copy(
            sources[which].at[:, lanes], inputs.at[n, which], load_sem.at[n, which]
        )

    def save(n, which):
        lanes = pl.ds(pl.multiple_of(n * chunk, chunk), chunk)
        rows = pl.ds(0, tokens if which == 0 else tokens - 16)
        return pltpu.make_async_copy(
            results.at[n, which, rows], outputs[which].at[rows, lanes], store_sem.at[n, which]
        )

    def save_tail(n, stream):
        lanes = pl.ds(pl.multiple_of(n * chunk, chunk), chunk)
        rows = pl.ds(tokens - 16, 16)
        return pltpu.make_async_copy(
            results.at[n, 1 + stream, rows],
            outputs[1 + stream].at[rows, lanes],
            tail_sem.at[n, stream],
        )

    def each(size, mine, action):
        for k in range(1, size):
            action(lax.rem(mine + k, size))

    def over(size, action):
        def body(k, carry):
            action(k)
            return carry

        lax.fori_loop(0, size, body, 0)

    def load_all(n):
        for which in (1, 2, 0, 3):
            load(n, which).start()

    over(steps, load_all)

    barrier = pltpu.get_barrier_semaphore()

    def greet(where):
        pl.semaphore_signal(barrier, inc=1, device_id=where, device_id_type=MESH)

    greet(device(after, row))
    greet(device(before, row))
    for k in range(1, planes):
        greet(in_plane(lax.rem(place + k, planes)))
    for k in range(1, depths):
        greet(in_depth(lax.rem(depth + k, depths)))

    starts = [jnp.int32(0)]
    for index in range(lengths.shape[1] - 1):
        starts.append(starts[-1] + lengths[0, index])

    def docs(positions):
        result = jnp.full(positions.shape, -1, jnp.int32)
        for start in starts:
            result = result + (positions >= start).astype(jnp.int32)
        return result

    def iota(shape, dim):
        return lax.broadcasted_iota(jnp.int32, shape, dim)

    anchor = me * tokens
    reach = tokens + 2 * HALO
    places[...] = docs(iota((reach, LANES), 0) + (anchor - HALO))
    own_docs = places[HALO : HALO + tokens]
    for offset in range(1, count_taps):
        prior_docs = places[HALO - offset : HALO - offset + tokens]
        feat_mask[offset - 1] = jnp.where(prior_docs == own_docs, 1.0, 0.0)
    spread = tokens + HALO
    here = iota((spread, LANES), 0) - HALO
    here_docs = places[0:spread]
    for offset in range(count_taps):
        there = here + offset
        fits = (there >= 0) & (there < tokens) & (places[offset : offset + spread] == here_docs)
        back_mask[offset] = jnp.where(fits, 1.0, 0.0)
    wide = (tokens, 2 * tokens)
    across = docs(iota((8, 3 * tokens), 1) + (anchor - tokens))[0:1]
    source_docs = jnp.broadcast_to(across[:, : 2 * tokens], wide)
    target_docs = jnp.broadcast_to(across[:, tokens:], wide)
    down = iota(wide, 0)
    side = iota(wide, 1)
    twice = jnp.concatenate([own_docs, own_docs], 1)
    lag = down - side + tokens
    fits = (twice == source_docs) & (lag >= 0) & (lag < tokens)
    conv_mask[...] = jnp.where(fits, 1.0, 0.0).astype(jnp.bfloat16)
    lag = side - down
    fits = (twice == target_docs) & (lag >= 0) & (lag < tokens)
    du_mask[...] = jnp.where(fits, 1.0, 0.0).astype(jnp.bfloat16)
    turned_docs = docs((anchor + tokens - 1) - iota((tokens, LANES), 0))
    twice = jnp.concatenate([turned_docs, turned_docs], 1)
    lag = 2 * tokens - 1 - down - side
    fits = (twice == source_docs) & (lag >= 0) & (lag < tokens)
    conv_keep[...] = jnp.where(fits, 1.0, 0.0)
    for stream in range(3):
        grads[stream, 0:HALO] = jnp.zeros((HALO, LANES), jnp.float32)
        grads[stream, HALO + tokens :] = jnp.zeros((HALO, LANES), jnp.float32)
    sums[...] = jnp.zeros(sums.shape, jnp.float32)
    packed[...] = jnp.zeros(packed.shape, jnp.float32)

    def clear(tile):
        for stream in range(3):
            window[tile, stream, 0:HALO] = jnp.zeros((HALO, LANES), jnp.float32)

    over(width // LANES, clear)
    lane_group = iota((tokens, LANES), 1) // group_width
    square = (LANES, LANES)
    turn = (iota(square, 0) + iota(square, 1)) % LANES == 0
    flipped[...] = jnp.dot(
        filters[...].astype(jnp.bfloat16),
        jnp.where(turn, 1.0, 0.0).astype(jnp.bfloat16),
        preferred_element_type=jnp.float32,
    )
    opposite = iota((tokens, LANES), 0) + iota((tokens, LANES), 1) == tokens - 1
    upside = jnp.where(opposite, 1.0, 0.0).astype(jnp.bfloat16)

    @pl.when(jnp.logical_not(has_prior))
    def _():
        u_prior[...] = jnp.zeros(u_prior.shape, u_prior.dtype)
        head_in[...] = jnp.zeros(head_in.shape, head_in.dtype)

    @pl.when(jnp.logical_not(has_next))
    def _():
        dz_next[...] = jnp.zeros(dz_next.shape, dz_next.dtype)
        back_in[...] = jnp.zeros(back_in.shape, back_in.dtype)

    def spot(i, stream):
        at = (i * 3 + stream) * margin
        return slice(at, at + margin)

    def stage_head(n):
        for which in (1, 2, 0):
            load(n, which).wait()
        for i in range(tiles):
            for stream in range(3):
                last = inputs[n, stream, tokens - 16 : tokens, i * LANES : (i + 1) * LANES]
                packed[spot(i, stream)] = last.astype(jnp.float32)[16 - margin :]
        head_out[n] = packed[...].astype(jnp.bfloat16)

    def send_head_on(n):
        @pl.when(has_next)
        def _():
            head_copy(n).start()

    def open_heads(n):
        packed[...] = head_in[n].astype(jnp.float32)
        for i in range(tiles):
            for stream in range(3):
                window[n * tiles + i, stream, HALO - margin : HALO] = packed[spot(i, stream)]

    def featurize(n, i):
        tile = n * tiles + i
        lanes = pl.ds(pl.multiple_of(tile * LANES, LANES), LANES)
        inner = pl.ds(pl.multiple_of(i * LANES, LANES), LANES)
        made = []
        for stream in range(3):
            own = inputs[n, stream, :, inner].astype(jnp.float32)
            window[tile, stream, HALO : HALO + tokens] = own
            own = own[EDGE:]
            result = taps[stream, 0:1, lanes] * own
            for offset in range(1, count_taps):
                start = HALO + EDGE - offset
                shifted = window[tile, stream, start : start + tokens - EDGE]
                result = result + taps[stream, offset : offset + 1, lanes] * (
                    shifted * feat_mask[offset - 1, EDGE:]
                )
            feats[tile, stream, EDGE:] = result
            made.append(result)
        u_own[n, EDGE:, inner] = (made[1] * made[2]).astype(jnp.bfloat16)
        gradient = inputs[n, 3, EDGE:, inner].astype(jnp.float32)
        dz_own[n, EDGE:, inner] = (gradient * made[0]).astype(jnp.bfloat16)

    def refine(n, i):
        tile = n * tiles + i
        lanes = pl.ds(pl.multiple_of(tile * LANES, LANES), LANES)
        inner = pl.ds(pl.multiple_of(i * LANES, LANES), LANES)
        made = []
        for stream in range(3):
            result = taps[stream, 0:1, lanes] * window[tile, stream, HALO : HALO + EDGE]
            for offset in range(1, count_taps):
                start = HALO - offset
                shifted = window[tile, stream, start : start + EDGE]
                result = result + taps[stream, offset : offset + 1, lanes] * (
                    shifted * feat_mask[offset - 1, 0:EDGE]
                )
            feats[tile, stream, 0:EDGE] = result
            made.append(result)
        u_own[n, 0:EDGE, inner] = (made[1] * made[2]).astype(jnp.bfloat16)
        gradient = inputs[n, 3, 0:EDGE, inner].astype(jnp.float32)
        dz_own[n, 0:EDGE, inner] = (gradient * made[0]).astype(jnp.bfloat16)

    def convolve(n, i):
        tile = n * tiles + i
        lanes = pl.ds(pl.multiple_of(tile * LANES, LANES), LANES)
        inner = pl.ds(pl.multiple_of(i * LANES, LANES), LANES)
        u_tile = u_own[n, :, inner]
        dz_tile = dz_own[n, :, inner]
        dz_turned = jnp.dot(upside, dz_tile, preferred_element_type=jnp.float32)
        dz_turned = dz_turned.astype(jnp.bfloat16)
        u_window = jnp.concatenate([u_prior[n, :, inner], u_tile], 0)
        dz_window = jnp.concatenate([dz_tile, dz_next[n, :, inner]], 0)
        conv = jnp.zeros((tokens, LANES), jnp.float32)
        du = jnp.zeros((tokens, LANES), jnp.float32)
        rows = pl.ds(pl.multiple_of(tile * per_tile, per_tile), per_tile)
        own_taps, own_flipped = filters[rows], flipped[rows]
        for group in range(per_tile):
            mine = lane_group == group

            def circulant(line):
                spread_line = jnp.broadcast_to(line[group : group + 1], (tokens, LANES))
                turned = pltpu.roll(spread_line, 0, 1, stride=1, stride_axis=0)
                half = turned.astype(jnp.bfloat16)
                return jnp.concatenate([half, half], 1)

            piece = jnp.dot(
                circulant(own_flipped) * conv_mask[...],
                u_window,
                preferred_element_type=jnp.float32,
            )
            conv = jnp.where(mine, piece, conv)
            piece = jnp.dot(
                circulant(own_taps) * du_mask[...],
                dz_window,
                preferred_element_type=jnp.float32,
            )
            du = jnp.where(mine, piece, du)
            chosen = jnp.where(mine, dz_turned, jnp.zeros_like(dz_turned))
            outer = lax.dot_general(
                chosen,
                u_window,
                (((1,), (1,)), ((), ())),
                preferred_element_type=jnp.float32,
            )
            outer = outer * conv_keep[...]
            folded = outer[:, :LANES] + outer[:, LANES:]
            turned = pltpu.roll(folded, 0, 1, stride=1, stride_axis=0)
            sums[24 + group : 25 + group] = jnp.sum(turned, axis=0, keepdims=True)
        u_float = u_tile.astype(jnp.float32)
        gradient = inputs[n, 3, :, inner].astype(jnp.float32)
        gain = skip[:, lanes]
        q_feat = feats[tile, 0]
        dz = gradient * q_feat
        total = conv + gain * u_float
        results[n, 0, :, inner] = (q_feat * total).astype(jnp.bfloat16)
        sums[count_taps : count_taps + 1] = jnp.sum(dz * u_float, axis=0, keepdims=True)
        du = du + gain * dz
        inside = pl.ds(HALO, tokens)
        grads[0, inside] = gradient * total
        grads[1, inside] = du * feats[tile, 2]
        grads[2, inside] = du * feats[tile, 1]
        for stream in range(3):
            result = None
            x_window = window[tile, stream]
            for offset in range(count_taps):
                shifted = grads[stream, offset : offset + tokens + HALO] * back_mask[offset]
                term = taps[stream, offset : offset + 1, lanes] * shifted
                result = term if result is None else result + term
                line = stream * 8 + offset
                sums[line : line + 1] = jnp.sum(shifted * x_window, axis=0, keepdims=True)
            heads[i, stream] = result[:HALO]
            tails[stream, :, lanes] = result[HALO + tokens - 16 :]
            whole = result[HALO : HALO + tokens - 16]
            results[n, 1 + stream, 0 : tokens - 16, inner] = whole.astype(jnp.bfloat16)
        partial[tile] = sums[...].astype(jnp.bfloat16)

        @pl.when(tile != place)
        def _():
            first(tile, place).start()

    def gather_own():
        gathered[place] = partial[place]
        each(planes, place, lambda peer: first(peer, peer).wait_recv())
        total = gathered[0].astype(jnp.float32)
        for index in range(1, planes):
            total = total + gathered[index].astype(jnp.float32)
        stacked[depth] = total.astype(jnp.bfloat16)
        each(depths, depth, lambda peer: second(peer, depth).start())

    def spread_own():
        each(depths, depth, lambda peer: second(peer, peer).wait_recv())
        total = stacked[0].astype(jnp.float32)
        for index in range(1, depths):
            total = total + stacked[index].astype(jnp.float32)
        spread_sums[place] = (total * scale).astype(jnp.bfloat16)
        each(planes, place, lambda peer: third(peer, place).start())

    def prepare(n):
        load(n, 3).wait()
        over(tiles, lambda i: featurize(n, i))

    over(LEAD, stage_head)
    over(EARLY, prepare)
    pl.semaphore_wait(barrier, planes + depths)
    over(LEAD, send_head_on)

    def step(n):
        @pl.when(n + LEAD < steps)
        def _():
            stage_head(n + LEAD)
            send_head_on(n + LEAD)

        @pl.when(n < steps)
        def _():
            @pl.when(n >= EARLY)
            def _():
                prepare(n)

            send_part(n, 0)

        ready = n - REFINE

        @pl.when((ready >= 0) & (ready < steps))
        def _():
            @pl.when(has_prior)
            def _():
                head_copy(ready).wait_recv()

            open_heads(ready)
            over(tiles, lambda i: refine(ready, i))
            send_part(ready, 1)

        past = n - AHEAD

        @pl.when(past >= 0)
        def _():
            @pl.when(has_prior)
            def _():
                u_copy(past, 0).wait_recv()
                u_copy(past, 1).wait_recv()

            @pl.when(has_next)
            def _():
                dz_copy(past, 0).wait_recv()
                dz_copy(past, 1).wait_recv()

            over(tiles, lambda i: convolve(past, i))
            packed[...] = jnp.zeros(packed.shape, jnp.float32)
            for i in range(tiles):
                for stream in range(3):
                    packed[spot(i, stream)] = heads[i, stream, HALO - margin : HALO]
            back_out[past] = packed[...].astype(jnp.bfloat16)

            for which in range(4):
                save(past, which).start()

            @pl.when(past == owned + 1)
            def _():
                gather_own()

            @pl.when(past == owned + 2)
            def _():
                spread_own()

    over(steps + AHEAD, step)

    @pl.when(owned == steps - 1)
    def _():
        gather_own()

    @pl.when(has_prior)
    def _():
        over(steps, lambda n: back_copy(n).start())

    @pl.when(owned >= steps - 2)
    def _():
        spread_own()

    def settle(n):
        @pl.when(has_next)
        def _():
            back_copy(n).wait_recv()

        packed[...] = back_in[n].astype(jnp.float32)
        for i in range(tiles):
            lanes = pl.ds(pl.multiple_of(n * chunk + i * LANES, LANES), LANES)
            for stream in range(3):
                tails[stream, 16 - margin : 16, lanes] += packed[spot(i, stream)]
                fixed = tails[stream, :, lanes].astype(jnp.bfloat16)
                results[n, 1 + stream, tokens - 16 : tokens, i * LANES : (i + 1) * LANES] = fixed
        for stream in range(3):
            save_tail(n, stream).start()

    def drain(n):
        for which in range(4):
            save(n, which).wait()
        for stream in range(3):
            save_tail(n, stream).wait()

        @pl.when(has_next)
        def _():
            head_copy(n).wait_send()
            u_copy(n, 0).wait_send()
            u_copy(n, 1).wait_send()

        @pl.when(has_prior)
        def _():
            dz_copy(n, 0).wait_send()
            dz_copy(n, 1).wait_send()
            back_copy(n).wait_send()

    over(steps, settle)
    over(steps, drain)
    each(planes, place, lambda peer: first(peer, place).wait_send())
    each(depths, depth, lambda peer: second(peer, depth).wait_send())
    each(planes, place, lambda peer: third(peer, peer).wait_recv())
    each(planes, place, lambda peer: third(peer, place).wait_send())


def finish_kernel(
    mixed_in,
    query_in,
    key_in,
    value_in,
    sums_in,
    mixed,
    grad_query,
    grad_key,
    grad_value,
    short_out,
    filters_out,
    skip_out,
    sums,
    short,
    filters,
    skip,
    opened,
    stage,
    loaded,
    copied,
    other,
):
    pairs = (mixed_in, mixed), (query_in, grad_query), (key_in, grad_key), (value_in, grad_value)
    parts = copied.shape[1]
    half = mixed.shape[0] // parts
    loads, saves = [], []
    for index, (given, out) in enumerate(pairs):
        for part in range(parts):
            rows = pl.ds(part * half, half)
            here = stage.at[index, rows]
            loads.append(pltpu.make_async_copy(given.at[rows], here, loaded.at[index, part]))
            saves.append(pltpu.make_async_copy(here, out.at[rows], copied.at[index, part]))
    first = pltpu.make_async_copy(sums_in, sums, other.at[0])
    first.start()
    for copy in loads:
        copy.start()
    tiles = sums.shape[0]
    count_taps = short.shape[1]
    per_tile = filters.shape[0] // tiles
    square = (LANES, LANES)
    turn = lax.broadcasted_iota(jnp.int32, square, 0) + lax.broadcasted_iota(jnp.int32, square, 1)
    turn = jnp.where(turn == LANES - 1, 1.0, 0.0).astype(jnp.bfloat16)

    first.wait()
    for i in range(tiles):
        lanes = slice(i * LANES, (i + 1) * LANES)
        opened[i] = sums[i].astype(jnp.float32)
        for stream in range(3):
            short[stream, :, lanes] = opened[i, stream * 8 : stream * 8 + count_taps]
        skip[:, lanes] = opened[i, count_taps : count_taps + 1]
        filters[i * per_tile : (i + 1) * per_tile] = jnp.dot(
            opened[i, 24:].astype(jnp.bfloat16), turn, preferred_element_type=jnp.float32
        )
    pieces = ((short, short_out), (filters, filters_out), (skip, skip_out))
    for index, (given, out) in enumerate(pieces):
        saves.append(pltpu.make_async_copy(given, out, other.at[1 + index]))
        saves[-1].start()
    for coming, leaving in zip(loads, saves):
        coming.wait()
        leaving.start()
    for copy in saves:
        copy.wait()


def local_block(scale, query, keys, values, cotangent, taps, filters, skip, lengths):
    steps = STEPS
    tokens, width = query.shape
    groups = filters.shape[0]
    chunk = width // steps
    tiles = width // LANES
    count_taps = taps.shape[1]
    spots = -(-3 * (count_taps - 1) * (chunk // LANES) // 16) * 16
    bf16, f32 = jnp.bfloat16, jnp.float32
    stream = jax.ShapeDtypeStruct((tokens, width), bf16)
    vmem = pl.BlockSpec(memory_space=pltpu.VMEM)
    hbm = pl.BlockSpec(memory_space=pl.ANY)
    dma = pltpu.SemaphoreType.DMA((steps,))
    pair = pltpu.SemaphoreType.DMA((steps, 2))
    plane = pltpu.SemaphoreType.DMA((32,))
    depth = pltpu.SemaphoreType.DMA((8,))
    piece = pltpu.VMEM((steps, tokens, chunk), bf16)
    margin = pltpu.VMEM((steps, spots, LANES), bf16)
    made = pl.pallas_call(
        functools.partial(block_kernel, steps, width // groups, scale),
        out_shape=[stream] * 4
        + [jax.ShapeDtypeStruct((tiles, 32, LANES), bf16)],
        in_specs=[pl.BlockSpec(memory_space=pltpu.SMEM)] + [hbm] * 4 + [vmem] * 3,
        out_specs=[hbm] * 4 + [vmem],
        scratch_shapes=[
            pltpu.VMEM((steps, 4, tokens, chunk), bf16),
            pltpu.VMEM((steps, 4, tokens, chunk), bf16),
            pltpu.VMEM((3, 16, width), f32),
            pltpu.VMEM((tiles, 3, tokens + HALO, LANES), f32),
            pltpu.VMEM((tiles, 3, tokens, LANES), f32),
            pltpu.VMEM((groups, LANES), f32),
            piece,
            piece,
            piece,
            piece,
            margin,
            margin,
            margin,
            margin,
            pltpu.VMEM((chunk // LANES, 3, HALO, LANES), f32),
            pltpu.VMEM((spots, LANES), f32),
            pltpu.VMEM((tokens + 2 * HALO, LANES), jnp.int32),
            pltpu.VMEM((count_taps - 1, tokens, LANES), f32),
            pltpu.VMEM((count_taps, tokens + HALO, LANES), f32),
            pltpu.VMEM((tokens, 2 * tokens), bf16),
            pltpu.VMEM((tokens, 2 * tokens), f32),
            pltpu.VMEM((tokens, 2 * tokens), bf16),
            pltpu.VMEM((3, tokens + 2 * HALO, LANES), f32),
            pltpu.VMEM((32, LANES), f32),
            pltpu.VMEM((tiles, 32, LANES), bf16),
            pltpu.VMEM((32, 32, LANES), bf16),
            pltpu.VMEM((8, 32, LANES), bf16),
            pltpu.SemaphoreType.DMA((steps, 4)),
            pltpu.SemaphoreType.DMA((steps, 4)),
            pltpu.SemaphoreType.DMA((steps, 3)),
        ]
        + [pair] * 4
        + [dma] * 4
        + [plane, plane, depth, depth, plane, plane],
        compiler_params=pltpu.CompilerParams(
            collective_id=0, has_side_effects=True, vmem_limit_bytes=56 * 2**20
        ),
        name="block",
    )(lengths, query, keys, values, cotangent, taps, filters, skip)
    return pl.pallas_call(
        finish_kernel,
        out_shape=[stream] * 4
        + [
            jax.ShapeDtypeStruct(taps.shape, f32),
            jax.ShapeDtypeStruct(filters.shape, f32),
            jax.ShapeDtypeStruct(skip.shape, f32),
        ],
        in_specs=[hbm] * 5,
        out_specs=[hbm] * 7,
        scratch_shapes=[
            pltpu.VMEM((tiles, 32, LANES), bf16),
            pltpu.VMEM(taps.shape, f32),
            pltpu.VMEM(filters.shape, f32),
            pltpu.VMEM(skip.shape, f32),
            pltpu.VMEM((tiles, 32, LANES), f32),
            pltpu.VMEM((4, tokens, width), bf16),
            pltpu.SemaphoreType.DMA((4, 4)),
            pltpu.SemaphoreType.DMA((4, 4)),
            pltpu.SemaphoreType.DMA((4,)),
        ],
        compiler_params=pltpu.CompilerParams(vmem_limit_bytes=60 * 2**20),
        name="finish",
    )(*made)


def shards(
    query_proj, key_proj, value_proj, short_taps, filter_taps, skip_gain, doc_lengths, out_grad
):
    tokens = query_proj.shape[1]
    scale = 1.0 / math.sqrt(tokens * lax.axis_size("ctx") * lax.axis_size("dp"))
    mixed, grad_query, grad_key, grad_value, short, filters, gain = local_block(
        scale,
        query_proj[0],
        key_proj[0],
        value_proj[0],
        out_grad[0],
        short_taps,
        filter_taps,
        skip_gain[None],
        doc_lengths,
    )
    return (
        mixed[None],
        grad_query[None],
        grad_key[None],
        grad_value[None],
        short,
        filters,
        gain[0],
    )


def solution(mesh):
    return jax.shard_map(
        shards,
        mesh=mesh,
        in_specs=(
            P("dp", "ctx", None),
            P("dp", "ctx", None),
            P("dp", "ctx", None),
            P(),
            P(),
            P(),
            P("dp", None),
            P("dp", "ctx", None),
        ),
        out_specs=(
            P("dp", "ctx", None),
            P("dp", "ctx", None),
            P("dp", "ctx", None),
            P("dp", "ctx", None),
            P(),
            P(),
            P(),
        ),
        check_vma=False,
    )
```

time: 123 us -> 104 us (0.85)
  local copies, waits for them, and re-layouts: 9.74 us -> 0 us
  Pallas kernels: 110 us -> 103 us
  other arithmetic: 1.73 us -> 0 us
    pallas_call x2, Pallas kernels: 110 us -> 103 us  [the longest x1 98.1 us: local_block(): pl.pallas_call(functools.partial(block_kernel, steps, width // groups, sc...]
    unnamed x16 -> x0, local copies, waits for them, and re-layouts: 7.09 us -> none
where the time goes in v2:
time: 104 us
  Pallas kernels  103 us (99%)
    pallas_call x1, Pallas kernels, local_block(): pl.pallas_call(functools.partial(block_kernel, steps, width // groups, sc...  98.1 us
    pallas_call x1, Pallas kernels, local_block(): pl.pallas_call(finish_kernel, out_shape=[stream] * 4 + [jax.ShapeDtypeStr...  4.96 us

profile of v2, /device:TPU:1, one launch (start us, length us, event | category | flops | bytes accessed | tf_op | source)
XLA Modules:
  0.0 103.7 jit_solution(9962946806492245178)
XLA Ops:
  0.6 98.1 %block.1 = (bf16[128,4096]{1,0:T(8,128)(2,1)}, bf16[128,4096]{1,0:T(8,128)(2,1)}, bf16[128,4096]{1,0:T(8,128)(2,1)}, bf16[128,4096]{1,0:T(8,128)(2,1)}, bf16[32,32,128]{2,1,0:T(8,128)(2,1)}) custom-call(s32[1,8]{1,0:T(1,128)} %lengths.1, bf16[128,4096]{1,0:T(8,128)(2,1)} %bitcast.10, bf16[128,4096]{1,0:T(8,128)(2,1)} %bitcast.11, ...), custom_call_target="tpu_custom_call" | custom-call | tf_op jit(solution)/shard_map/block/pallas_call | solution.py:674
  98.7 5.0 %finish.1 = (bf16[128,4096]{1,0:T(8,128)(2,1)}, bf16[128,4096]{1,0:T(8,128)(2,1)}, bf16[128,4096]{1,0:T(8,128)(2,1)}, bf16[128,4096]{1,0:T(8,128)(2,1)}, f32[3,7...) custom-call(bf16[128,4096]{1,0:T(8,128)(2,1)} %get-tuple-element.19.mixed_in, ...), custom_call_target="tpu_custom_call" | custom-call | tf_op jit(solution)/shard_map/finish/pallas_call | solution.py:720

commit v3 on v2

--- a/solution.py
+++ b/solution.py
@@ -12,7 +12,7 @@
 LANES = 128
 HALO = 8
 STEPS = 8
-AHEAD = 3
+OUTER, INNER = 3, 4
 LEAD = 2
 EARLY = 2
 EDGE = 16
@@ -106,6 +106,7 @@
     planes = gathered.shape[0]
     depths = stacked.shape[0]
     owned = place // tiles
+    ahead = jnp.where((low == 0) | (low == 3), OUTER, INNER)
 
     def in_plane(index):
         return device(
@@ -130,20 +131,26 @@
             head_out.at[n], head_in.at[n], send_head.at[n], recv_head.at[n], device(after, row)
         )
 
-    parts = (pl.ds(EDGE, tokens - EDGE), pl.ds(0, EDGE))
+    main = pl.ds(EDGE, tokens - EDGE)
+    half = chunk // 2
+    parts = (
+        (main, pl.ds(0, half)),
+        (pl.ds(0, EDGE), pl.ds(0, chunk)),
+        (main, pl.ds(half, half)),
+    )
 
     def u_copy(n, part):
-        rows = parts[part]
+        rows, lanes = parts[part]
         return remote(
-            u_own.at[n, rows], u_prior.at[n, rows], send_u.at[n, part], recv_u.at[n, part],
-            device(after, row),
+            u_own.at[n, rows, lanes], u_prior.at[n, rows, lanes], send_u.at[n, part],
+            recv_u.at[n, part], device(after, row),
         )
 
     def dz_copy(n, part):
-        rows = parts[part]
+        rows, lanes = parts[part]
         return remote(
-            dz_own.at[n, rows], dz_next.at[n, rows], send_dz.at[n, part], recv_dz.at[n, part],
-            device(before, row),
+            dz_own.at[n, rows, lanes], dz_next.at[n, rows, lanes], send_dz.at[n, part],
+            recv_dz.at[n, part], device(before, row),
         )
 
     def send_part(n, part):
@@ -286,6 +293,7 @@
 
     over(width // LANES, clear)
     lane_group = iota((tokens, LANES), 1) // group_width
+    lane_group_twice = jnp.concatenate([lane_group, lane_group], 0)
     square = (LANES, LANES)
     turn = (iota(square, 0) + iota(square, 1)) % LANES == 0
     flipped[...] = jnp.dot(
@@ -381,34 +389,33 @@
         dz_turned = dz_turned.astype(jnp.bfloat16)
         u_window = jnp.concatenate([u_prior[n, :, inner], u_tile], 0)
         dz_window = jnp.concatenate([dz_tile, dz_next[n, :, inner]], 0)
-        conv = jnp.zeros((tokens, LANES), jnp.float32)
-        du = jnp.zeros((tokens, LANES), jnp.float32)
+        zero = jnp.zeros((), jnp.bfloat16)
         rows = pl.ds(pl.multiple_of(tile * per_tile, per_tile), per_tile)
         own_taps, own_flipped = filters[rows], flipped[rows]
-        for group in range(per_tile):
-            mine = lane_group == group
-
-            def circulant(line):
-                spread_line = jnp.broadcast_to(line[group : group + 1], (tokens, LANES))
-                turned = pltpu.roll(spread_line, 0, 1, stride=1, stride_axis=0)
-                half = turned.astype(jnp.bfloat16)
-                return jnp.concatenate([half, half], 1)
-
-            piece = jnp.dot(
-                circulant(own_flipped) * conv_mask[...],
-                u_window,
+
+        def circulant(line, mask):
+            turned = jnp.broadcast_to(line, (tokens, LANES))
+            turned = pltpu.roll(turned, 0, 1, stride=1, stride_axis=0).astype(jnp.bfloat16)
+            return jnp.concatenate([turned, turned], 1) * mask[...]
+
+        def pick(group, value):
+            picks = lane_group if value.shape[0] == tokens else lane_group_twice
+            return jnp.where(picks == group, value, zero)
+
+        def convolved(lines, mask, value):
+            left = [circulant(lines[g : g + 1], mask) for g in range(per_tile)]
+            right = [pick(g, value) for g in range(per_tile)]
+            return jnp.dot(
+                jnp.concatenate(left, 1),
+                jnp.concatenate(right, 0),
                 preferred_element_type=jnp.float32,
             )
-            conv = jnp.where(mine, piece, conv)
-            piece = jnp.dot(
-                circulant(own_taps) * du_mask[...],
-                dz_window,
-                preferred_element_type=jnp.float32,
-            )
-            du = jnp.where(mine, piece, du)
-            chosen = jnp.where(mine, dz_turned, jnp.zeros_like(dz_turned))
+
+        conv = convolved(own_flipped, conv_mask, u_window)
+        du = convolved(own_taps, du_mask, dz_window)
+        for group in range(per_tile):
             outer = lax.dot_general(
-                chosen,
+                pick(group, dz_turned),
                 u_window,
                 (((1,), (1,)), ((), ())),
                 preferred_element_type=jnp.float32,
@@ -488,6 +495,7 @@
                 prepare(n)
 
             send_part(n, 0)
+            send_part(n, 2)
 
         ready = n - REFINE
 
@@ -501,9 +509,9 @@
             over(tiles, lambda i: refine(ready, i))
             send_part(ready, 1)
 
-        past = n - AHEAD
-
-        @pl.when(past >= 0)
+        past = n - ahead
+
+        @pl.when((past >= 0) & (past < steps))
         def _():
             @pl.when(has_prior)
             def _():
@@ -515,7 +523,18 @@
                 dz_copy(past, 0).wait_recv()
                 dz_copy(past, 1).wait_recv()
 
-            over(tiles, lambda i: convolve(past, i))
+            def one(i):
+                @pl.when((i == tiles // 2) & has_prior)
+                def _():
+                    u_copy(past, 2).wait_recv()
+
+                @pl.when((i == tiles // 2) & has_next)
+                def _():
+                    dz_copy(past, 2).wait_recv()
+
+                convolve(past, i)
+
+            over(tiles, one)
             packed[...] = jnp.zeros(packed.shape, jnp.float32)
             for i in range(tiles):
                 for stream in range(3):
@@ -525,17 +544,17 @@
             for which in range(4):
                 save(past, which).start()
 
-            @pl.when(past == owned + 1)
+            @pl.when(past == owned + 2)
             def _():
                 gather_own()
 
-            @pl.when(past == owned + 2)
+            @pl.when(past == owned + 3)
             def _():
                 spread_own()
 
-    over(steps + AHEAD, step)
-
-    @pl.when(owned == steps - 1)
+    over(steps + max(OUTER, INNER), step)
+
+    @pl.when(owned >= steps - 2)
     def _():
         gather_own()
 
@@ -543,7 +562,7 @@
     def _():
         over(steps, lambda n: back_copy(n).start())
 
-    @pl.when(owned >= steps - 2)
+    @pl.when(owned >= steps - 3)
     def _():
         spread_own()
 
@@ -573,19 +592,21 @@
             head_copy(n).wait_send()
             u_copy(n, 0).wait_send()
             u_copy(n, 1).wait_send()
+            u_copy(n, 2).wait_send()
 
         @pl.when(has_prior)
         def _():
             dz_copy(n, 0).wait_send()
             dz_copy(n, 1).wait_send()
+            dz_copy(n, 2).wait_send()
             back_copy(n).wait_send()
 
     over(steps, settle)
     over(steps, drain)
     each(planes, place, lambda peer: first(peer, place).wait_send())
     each(depths, depth, lambda peer: second(peer, depth).wait_send())
+    each(planes, place, lambda peer: third(peer, place).wait_send())
     each(planes, place, lambda peer: third(peer, peer).wait_recv())
-    each(planes, place, lambda peer: third(peer, place).wait_send())
 
 
 def finish_kernel(
@@ -666,7 +687,7 @@
     vmem = pl.BlockSpec(memory_space=pltpu.VMEM)
     hbm = pl.BlockSpec(memory_space=pl.ANY)
     dma = pltpu.SemaphoreType.DMA((steps,))
-    pair = pltpu.SemaphoreType.DMA((steps, 2))
+    pair = pltpu.SemaphoreType.DMA((steps, 3))
     plane = pltpu.SemaphoreType.DMA((32,))
     depth = pltpu.SemaphoreType.DMA((8,))
     piece = pltpu.VMEM((steps, tokens, chunk), bf16)

time: 104 us -> 98.3 us (0.945)
  Pallas kernels: 103 us -> 97.5 us
    pallas_call x1, Pallas kernels: 98.1 us -> 92.6 us  [local_block(): pl.pallas_call(functools.partial(block_kernel, steps, width // groups, sc...]
where the time goes in v3:
time: 98.3 us; the launch traced here: 98.2 us
  Pallas kernels  97.5 us (99%)
    pallas_call x1, Pallas kernels, local_block(): pl.pallas_call(functools.partial(block_kernel, steps, width // groups, sc...  92.6 us
    pallas_call x1, Pallas kernels, local_block(): pl.pallas_call(finish_kernel, out_shape=[stream] * 4 + [jax.ShapeDtypeStr...  4.96 us

profile of v3, /device:TPU:1, one launch (start us, length us, event | category | flops | bytes accessed | tf_op | source)
XLA Modules:
  0.0 98.2 jit_solution(16215162331326004946)
XLA Ops:
  0.6 92.6 %block.1 = (bf16[128,4096]{1,0:T(8,128)(2,1)}, bf16[128,4096]{1,0:T(8,128)(2,1)}, bf16[128,4096]{1,0:T(8,128)(2,1)}, bf16[128,4096]{1,0:T(8,128)(2,1)}, bf16[32,32,128]{2,1,0:T(8,128)(2,1)}) custom-call(s32[1,8]{1,0:T(1,128)} %lengths.1, bf16[128,4096]{1,0:T(8,128)(2,1)} %bitcast.10, bf16[128,4096]{1,0:T(8,128)(2,1)} %bitcast.11, ...), custom_call_target="tpu_custom_call" | custom-call | tf_op jit(solution)/shard_map/block/pallas_call | solution.py:695
  93.2 5.0 %finish.1 = (bf16[128,4096]{1,0:T(8,128)(2,1)}, bf16[128,4096]{1,0:T(8,128)(2,1)}, bf16[128,4096]{1,0:T(8,128)(2,1)}, bf16[128,4096]{1,0:T(8,128)(2,1)}, f32[3,7...) custom-call(bf16[128,4096]{1,0:T(8,128)(2,1)} %get-tuple-element.19.mixed_in, ...), custom_call_target="tpu_custom_call" | custom-call | tf_op jit(solution)/shard_map/finish/pallas_call | solution.py:741

commit v4 on v3

--- a/solution.py
+++ b/solution.py
@@ -32,14 +32,18 @@
     keys,
     values,
     cotangent,
-    taps,
-    filters,
-    skip,
+    taps_in,
+    filters_in,
+    skip_in,
     mixed,
     grad_query,
     grad_key,
     grad_value,
     spread_sums,
+    taps,
+    filters,
+    skip,
+    param_sem,
     inputs,
     results,
     tails,
@@ -222,7 +226,12 @@
         for which in (1, 2, 0, 3):
             load(n, which).start()
 
-    over(steps, load_all)
+    params = [
+        pltpu.make_async_copy(given, held, param_sem.at[index])
+        for index, (given, held) in enumerate(
+            ((taps_in, taps), (filters_in, filters), (skip_in, skip))
+        )
+    ]
 
     barrier = pltpu.get_barrier_semaphore()
 
@@ -236,6 +245,9 @@
     for k in range(1, depths):
         greet(in_depth(lax.rem(depth + k, depths)))
 
+    for copy in params:
+        copy.start()
+    over(steps, load_all)
     starts = [jnp.int32(0)]
     for index in range(lengths.shape[1] - 1):
         starts.append(starts[-1] + lengths[0, index])
@@ -296,6 +308,8 @@
     lane_group_twice = jnp.concatenate([lane_group, lane_group], 0)
     square = (LANES, LANES)
     turn = (iota(square, 0) + iota(square, 1)) % LANES == 0
+    for copy in params:
+        copy.wait()
     flipped[...] = jnp.dot(
         filters[...].astype(jnp.bfloat16),
         jnp.where(turn, 1.0, 0.0).astype(jnp.bfloat16),
@@ -441,7 +455,9 @@
             result = None
             x_window = window[tile, stream]
             for offset in range(count_taps):
-                shifted = grads[stream, offset : offset + tokens + HALO] * back_mask[offset]
+                shifted = grads[stream, offset : offset + tokens + HALO]
+                if offset:
+                    shifted = shifted * back_mask[offset]
                 term = taps[stream, offset : offset + 1, lanes] * shifted
                 result = term if result is None else result + term
                 line = stream * 8 + offset
@@ -696,9 +712,13 @@
         functools.partial(block_kernel, steps, width // groups, scale),
         out_shape=[stream] * 4
         + [jax.ShapeDtypeStruct((tiles, 32, LANES), bf16)],
-        in_specs=[pl.BlockSpec(memory_space=pltpu.SMEM)] + [hbm] * 4 + [vmem] * 3,
+        in_specs=[pl.BlockSpec(memory_space=pltpu.SMEM)] + [hbm] * 7,
         out_specs=[hbm] * 4 + [vmem],
         scratch_shapes=[
+            pltpu.VMEM(taps.shape, f32),
+            pltpu.VMEM(filters.shape, f32),
+            pltpu.VMEM(skip.shape, f32),
+            pltpu.SemaphoreType.DMA((3,)),
             pltpu.VMEM((steps, 4, tokens, chunk), bf16),
             pltpu.VMEM((steps, 4, tokens, chunk), bf16),
             pltpu.VMEM((3, 16, width), f32),

time: 98.3 us -> 98 us (level)
  no operation moved by 1% of the time
where the time goes in v4:
time: 98 us; the launch traced here: 97.9 us
  Pallas kernels  97.2 us (99%)
    pallas_call x1, Pallas kernels, local_block(): pl.pallas_call(functools.partial(block_kernel, steps, width // groups, sc...  92.3 us
    pallas_call x1, Pallas kernels, local_block(): pl.pallas_call(finish_kernel, out_shape=[stream] * 4 + [jax.ShapeDtypeStr...  4.96 us

profile of v4, /device:TPU:1, one launch (start us, length us, event | category | flops | bytes accessed | tf_op | source)
XLA Modules:
  0.0 97.9 jit_solution(1312043600096865798)
XLA Ops:
  0.6 92.3 %block.1 = (bf16[128,4096]{1,0:T(8,128)(2,1)}, bf16[128,4096]{1,0:T(8,128)(2,1)}, bf16[128,4096]{1,0:T(8,128)(2,1)}, bf16[128,4096]{1,0:T(8,128)(2,1)}, bf16[32,32,128]{2,1,0:T(8,128)(2,1)}) custom-call(s32[1,8]{1,0:T(1,128)} %lengths.1, bf16[128,4096]{1,0:T(8,128)(2,1)} %bitcast.10, bf16[128,4096]{1,0:T(8,128)(2,1)} %bitcast.11, ...), custom_call_target="tpu_custom_call" | custom-call | tf_op jit(solution)/shard_map/block/pallas_call | solution.py:711
  92.9 5.0 %finish.1 = (bf16[128,4096]{1,0:T(8,128)(2,1)}, bf16[128,4096]{1,0:T(8,128)(2,1)}, bf16[128,4096]{1,0:T(8,128)(2,1)}, bf16[128,4096]{1,0:T(8,128)(2,1)}, f32[3,7...) custom-call(bf16[128,4096]{1,0:T(8,128)(2,1)} %get-tuple-element.19.mixed_in, ...), custom_call_target="tpu_custom_call" | custom-call | tf_op jit(solution)/shard_map/finish/pallas_call | solution.py:761
